TPU v7x, 32 devices: a whole 2x2x4 slice. The times are simulated.
32 devices in a mesh: pool: 8 (over y, x, core), tp: 4 (over z).
Axes of the slice: x: 2, y: 2, z: 4, core: 2. Of those that a mesh axis runs over, the one named last changes fastest.
Arguments:
- projected_mixer: bfloat16 [256, 4, 8192], P('pool', None, 'tp'), may hold values from -6 to 6
- projected_gate: bfloat16 [256, 4, 8192], P('pool', None, 'tp'), may hold values from -6 to 6
- slot_state_cache: bfloat16 [512, 19, 8192], P('pool', None, 'tp'), may hold values from -6 to 6
- session_holder: int32 [256], P('pool'), may hold values from 0 to 7, as said below
- session_slot: int32 [256], P('pool'), may hold values from 0 to 63, as said below
- conversation_customer: int32 [256], P('pool'), may hold values from 0 to 63
- filter_tap_weight: float32 [4, 8192], P(None, 'tp'), may hold values from -3 to 3
- filter_bias: float32 [8192], P('tp'), may hold values from -3 to 3
- lowrank_step_weight: bfloat16 [8192, 512], P('tp'), may hold values from -0.0625 to 0.0625
- state_maps_weight: bfloat16 [8192, 32], P('tp'), may hold values from -0.0625 to 0.0625
- adapter_down_maps: bfloat16 [8192, 1024], P('tp'), may hold values from -0.0625 to 0.0625
- adapter_up_maps: bfloat16 [1024, 512], replicated, may hold values from -1.5 to 1.5
- step_size_gain: float32 [512], replicated, may hold values from 0.5 to 1.5
- step_up_weight: bfloat16 [512, 8192], P(None, 'tp'), may hold values from -0.25 to 0.25
- step_size_bias: float32 [8192], P('tp'), may hold values from -4 to -1
- log_decay_rates: float32 [16, 8192], P(None, 'tp'), may hold values from 0 to 2.77
- skip_factor: float32 [8192], P('tp'), may hold values from 0.5 to 1.5
Outputs:
- gated_out: bfloat16 [256, 4, 8192], P('pool', None, 'tp')
- new_cache: bfloat16 [512, 19, 8192], P('pool', None, 'tp')
Inputs may be any that keep to these rules, and one draw needn't show every extreme that they name: `session_holder`: within the 32 rows of one index of pool, no owner is named by more than 8 rows. `session_slot`: no two rows name the same owner and slot.
All inputs are finite; a program needn't handle non-finite values.
Results may differ from a plain program's by a relative error of at most 0.0055.
Values may be sent and summed in bfloat16 or wider, within the bound.
A program may use at most 128 MiB of HBM per device.

v0:
```python
import jax
import jax.numpy as jnp
from jax import lax
from jax.sharding import PartitionSpec as P

STATE = 16
ADAPTER_RANK = 16
TENANT_COUNT = 64


def one_hot_rows(index_list, count):
    return (index_list[:, None] == jnp.arange(count, dtype=jnp.int32)[None, :]).astype(jnp.bfloat16)


def take_rows(table, index_list):
    flattened = table.reshape(table.shape[0], -1)
    selector = one_hot_rows(index_list, table.shape[0])
    picked = jnp.dot(selector, flattened, preferred_element_type=jnp.float32).astype(table.dtype)
    return picked.reshape((index_list.shape[0],) + table.shape[1:])


def place_rows(values, index_list, count):
    flattened = values.reshape(values.shape[0], -1)
    selector = one_hot_rows(index_list, count)
    placed = jnp.dot(selector.T, flattened, preferred_element_type=jnp.float32).astype(values.dtype)
    return placed.reshape((count,) + values.shape[1:])


def write_rows(table, values, index_list):
    count = table.shape[0]
    placed = place_rows(values, index_list, count)
    reached = jnp.any(index_list[:, None] == jnp.arange(count, dtype=jnp.int32)[None, :], axis=0)
    return jnp.where(reached[:, None, None], placed, table)


def place_ints(values, index_list, count, filler):
    matches = index_list[:, None] == jnp.arange(count, dtype=jnp.int32)[None, :]
    summed = jnp.sum(jnp.where(matches, (values - filler)[:, None], 0), axis=0)
    return summed + filler


def mixer_rows(
    mixer_inputs,
    switch_arguments,
    saved_state,
    tenant_list,
    filter_tap_weight,
    filter_bias,
    lowrank_step_weight,
    state_maps_weight,
    adapter_down_maps,
    adapter_up_maps,
    step_size_gain,
    step_up_weight,
    step_size_bias,
    log_decay_rates,
    skip_factor,
):
    row_count, step_count, chan_count = mixer_inputs.shape
    window = jnp.concatenate([saved_state[:, STATE:, :], mixer_inputs], axis=1)
    conv_sum = filter_bias[None, None, :] + jnp.zeros(
        (row_count, step_count, chan_count), jnp.float32
    )
    for tap_idx in range(filter_tap_weight.shape[0]):
        conv_sum = conv_sum + filter_tap_weight[tap_idx][None, None, :] * window[
            :, tap_idx : tap_idx + step_count, :
        ].astype(jnp.float32)
    activated = jax.nn.silu(conv_sum).astype(jnp.bfloat16)
    flattened_rows = activated.reshape(row_count * step_count, chan_count)
    part_low = jnp.dot(flattened_rows, lowrank_step_weight, preferred_element_type=jnp.float32)
    part_maps = jnp.dot(flattened_rows, state_maps_weight, preferred_element_type=jnp.float32)
    every_adapter = jnp.dot(flattened_rows, adapter_down_maps, preferred_element_type=jnp.float32)
    tenant_flat = jnp.repeat(tenant_list, step_count)
    selected_rows = jnp.arange(TENANT_COUNT, dtype=jnp.int32)[None, :] == tenant_flat[:, None]
    part_adapt = jnp.sum(
        jnp.where(
            selected_rows[:, :, None], every_adapter.reshape(-1, TENANT_COUNT, ADAPTER_RANK), 0.0
        ),
        axis=1,
    )
    lowrank_sum, mapped, adapter_applied = lax.psum((part_low, part_maps, part_adapt), "tp")
    adapter_middle = (
        jnp.where(selected_rows[:, :, None], adapter_applied[:, None, :], 0.0)
        .reshape(-1, TENANT_COUNT * ADAPTER_RANK)
        .astype(jnp.bfloat16)
    )
    adapter_term = jnp.dot(adapter_middle, adapter_up_maps, preferred_element_type=jnp.float32)
    before_norm = lowrank_sum + adapter_term
    mean_sq = jnp.mean(before_norm * before_norm, axis=1, keepdims=True)
    normed = (before_norm / jnp.sqrt(mean_sq + 1e-06) * step_size_gain[None, :]).astype(
        jnp.bfloat16
    )
    delta = jax.nn.softplus(
        jnp.dot(normed, step_up_weight, preferred_element_type=jnp.float32)
        + step_size_bias[None, :]
    )
    delta = delta.reshape(row_count, step_count, chan_count)
    maps_in = mapped[:, :STATE].reshape(row_count, step_count, STATE)
    maps_out = mapped[:, STATE:].reshape(row_count, step_count, STATE)
    decay_base = -jnp.exp(log_decay_rates)
    act_wide = activated.astype(jnp.float32)
    state_now = saved_state[:, :STATE, :].astype(jnp.float32)
    collected = []
    for step_idx in range(step_count):
        decay_rate = jnp.exp(delta[:, step_idx, None, :] * decay_base[None, :, :])
        driven = (delta[:, step_idx, :] * act_wide[:, step_idx, :])[:, None, :] * maps_in[
            :, step_idx, :, None
        ]
        state_now = decay_rate * state_now + driven
        output_now = (
            jnp.sum(maps_out[:, step_idx, :, None] * state_now, axis=1)
            + skip_factor[None, :] * act_wide[:, step_idx, :]
        )
        output_now = output_now * jax.nn.silu(switch_arguments[:, step_idx, :].astype(jnp.float32))
        collected.append(output_now)
    gated_result = jnp.stack(collected, axis=1).astype(jnp.bfloat16)
    newest_state = jnp.concatenate(
        [state_now.astype(jnp.bfloat16), window[:, step_count:, :]], axis=1
    )
    return (gated_result, newest_state)


def local(
    projected_mixer,
    projected_gate,
    slot_state_cache,
    session_holder,
    session_slot,
    conversation_customer,
    filter_tap_weight,
    filter_bias,
    lowrank_step_weight,
    state_maps_weight,
    adapter_down_maps,
    adapter_up_maps,
    step_size_gain,
    step_up_weight,
    step_size_bias,
    log_decay_rates,
    skip_factor,
):
    owners = lax.axis_size("pool")
    slot_count, depth_rows, chan_count = slot_state_cache.shape
    per_owner = slot_count // owners
    slots_each = owners * per_owner
    owner_match = (session_holder[:, None] == jnp.arange(owners, dtype=jnp.int32)[None, :]).astype(
        jnp.int32
    )
    owner_rank = jnp.sum((jnp.cumsum(owner_match, axis=0) - 1) * owner_match, axis=1)
    target = session_holder * per_owner + owner_rank
    request_slot = place_ints(session_slot, target, slots_each, -1)
    weights = (
        filter_tap_weight,
        filter_bias,
        lowrank_step_weight,
        state_maps_weight,
        adapter_down_maps,
        adapter_up_maps,
        step_size_gain,
        step_up_weight,
        step_size_bias,
        log_decay_rates,
        skip_factor,
    )
    asked_slot = lax.all_to_all(
        request_slot.reshape(owners, per_owner), "pool", split_axis=0, concat_axis=0, tiled=True
    ).reshape(slots_each)
    picked = take_rows(slot_state_cache, asked_slot)
    arrived = lax.all_to_all(
        picked.reshape(owners, per_owner, depth_rows, chan_count),
        "pool",
        split_axis=0,
        concat_axis=0,
        tiled=True,
    )
    saved_state = take_rows(arrived.reshape(slots_each, depth_rows, chan_count), target)
    gated_result, newest_state = mixer_rows(
        projected_mixer, projected_gate, saved_state, conversation_customer, *weights
    )
    outgoing = place_rows(newest_state, target, slots_each)
    came_back = lax.all_to_all(
        outgoing.reshape(owners, per_owner, depth_rows, chan_count),
        "pool",
        split_axis=0,
        concat_axis=0,
        tiled=True,
    )
    new_cache = write_rows(
        slot_state_cache, came_back.reshape(slots_each, depth_rows, chan_count), asked_slot
    )
    return (gated_result, new_cache)


def solution(mesh):
    placed = (
        P("pool", None, "tp"),
        P("pool", None, "tp"),
        P("pool", None, "tp"),
        P("pool"),
        P("pool"),
        P("pool"),
        P(None, "tp"),
        P("tp"),
        P("tp", None),
        P("tp", None),
        P("tp", None),
        P(),
        P(),
        P(None, "tp"),
        P("tp"),
        P(None, "tp"),
        P("tp"),
    )
    return jax.shard_map(
        local,
        mesh=mesh,
        in_specs=placed,
        out_specs=(P("pool", None, "tp"), P("pool", None, "tp")),
        check_vma=False,
    )
```

profile of v0, /device:TPU:0, one launch (start us, length us, event | category | flops | bytes accessed | tf_op | source)
XLA Modules:
  0.0 298.3 jit_solution(8503171981174317748)
XLA Ops:
  10.4 5.2 %all-to-all-start = ((s32[8,1,8]{2,1,0:T(1,128)}), s32[8,1,8]{2,1,0:T(1,128)S(1)}, u32[]{:S(2)}, u32[]{:S(2)}) async-start(s32[8,1,8]{2,1,0:T(1,128)} %bitcast.1), calls=%async_computation | async-start | bytes 8192 | tf_op jit(solution)/shard_map/all_to_all | solution.py:165
  15.6 5.5 %copy.194 = bf16[19,8,8,2048]{3,2,0,1:T(8,128)(2,1)} copy(bf16[19,8,8,2048]{3,2,1,0:T(8,128)(2,1)} %bitcast.79) | data formatting | bytes 9961472 | tf_op jit(solution)/shard_map/reshape | solution.py:16
  22.3 6.1 %convolution_convert_fusion.2 = bf16[64,38912]{1,0:T(8,128)(2,1)} fusion(bf16[64,38912]{1,0:T(8,128)(2,1)} %bitcast.81, s32[64]{0:T(128)S(1)} %eq.38), kind=kOutput, calls=%fused_computation.2 | convolution fusion | flops 321261568 | bytes 9961728 | tf_op jit(solution)/shard_map/dot_general | solution.py:18
  28.5 4.6 %all-to-all-start.1 = ((bf16[8,8,19,2048]{3,1,2,0:T(8,128)(2,1)}), bf16[8,8,19,2048]{3,1,2,0:T(8,128)(2,1)}, u32[]{:S(2)}, u32[]{:S(2)}) async-start(bf16[8,8,19,2048]{3,1,2,0:T(8,128)(2,1)} %bitcast.80), calls=%async_computation.1 | async-start | bytes 9961472 | tf_op jit(solution)/shard_map/all_to_all | solution.py:169
  33.2 6.5 %copy.149 = bf16[2048,1024]{0,1:T(8,128)(2,1)} copy(bf16[2048,1024]{1,0:T(8,128)(2,1)} %param.27) | data formatting | bytes 8388608 | tf_op args[10]
  41.1 49.5 %all-to-all-done.1 = bf16[8,8,19,2048]{3,1,2,0:T(8,128)(2,1)} async-done(((bf16[8,8,19,2048]{3,1,2,0:T(8,128)(2,1)}), bf16[8,8,19,2048]{3,1,2,0:T(8,128)(2,1)}, u32[]{:S(2)}, u32[]{:S(2)}) %all-to-all-start.1) | async-done | bytes 4980768 | tf_op jit(solution)/shard_map/all_to_all | solution.py:169
  90.6 4.8 %convolution_convert_fusion.3 = bf16[32,38912]{1,0:T(8,128)(2,1)} fusion(bf16[64,38912]{1,0:T(8,128)(2,1)} %bitcast.3, s32[32]{0:T(128)S(1)} %get-tuple-element.54), kind=kOutput, calls=%fused_computation.3 | convolution fusion | flops 160630784 | bytes 7471232 | tf_op jit(solution)/shard_map/dot_general | solution.py:18
  95.5 4.8 %reshape.130 = bf16[32,19,2048]{2,1,0:T(8,128)(2,1)} reshape(bf16[32,38912]{1,0:T(8,128)(2,1)} %convolution_convert_fusion.3) | data formatting | bytes 4980736 | tf_op jit(solution)/shard_map/reshape | solution.py:19
  105.2 2.0 reshape.131
  107.3 2.0 reshape.137
  110.6 6.9 %fusion.5 = f32[128,16]{0,1:T(8,128)S(1)} fusion(bf16[128,2048,1]{1,0,2:T(8,128)(2,1)} %reshape.137, bf16[64,16,2048]{2,1,0:T(8,128)(2,1)} %bitcast.85, pred[128,64]{0,1:T(8,128)(4,1)S(1)} %iota_compare_fusion), kind=kOutput, calls=%fused_computation.20 | convolution fusion | flops 537131008 | bytes 4734976 | tf_op jit(solution)/shard_map/dot_general | solution.py:72
  117.5 19.2 %all-reduce = (f32[128,32]{0,1:T(8,128)S(1)}, bf16[128,16]{0,1:T(8,128)(2,1)S(1)}) all-reduce(f32[128,32]{0,1:T(8,128)S(1)} %fusion.44, f32[128,16]{0,1:T(8,128)S(1)} %fusion.5), channel_id=1, replica_groups=mesh['pool'=8,'tp'=4] {'tp'}, use_global_device_ids=true, to_apply=%region_3.4 | all-reduce | flops 6144 | bytes 45056 | tf_op jit(solution)/shard_map/psum | solution.py:81
  137.5 2.9 fusion.45
  144.4 27.9 %all-reduce.3.cloned.1.call-done = f32[128,512]{1,0:T(8,128)} async-done(((f32[128,512]{1,0:T(8,128)}), f32[128,512]{1,0:T(8,128)}) %all-reduce.3.cloned.1.call-update) | async-done | bytes 262160 | tf_op jit(solution)/shard_map/psum | solution.py:81
  174.0 2.6 compare_select_fusion
  180.1 7.9 %multiply_reduce_fusion.1 = (f32[32,2048]{1,0:T(8,128)}, f32[32,2048]{1,0:T(8,128)}, f32[32,2048]{1,0:T(8,128)}, bf16[32,16,2048]{2,1,0:T(8,128)(2,1)S(1)}) fusion(f32[32,16]{1,0:T(8,128)S(1)} %bitcast.97, f32[32,2048]{1,0:T(8,128)S(1)} %get-tuple-element.23, f32[32,2048]{1,0:T(8,128)S(1)} %get-tuple-element.36, f32[32,16]{1,0:T(8,128)S(1)} %bitcast.100, ...), kind=kLoop, calls=%fused_computation.9 | loop fusion | flops 24969216 | bytes 7223296 | tf_op jit(solution)/shard_map/reduce_sum | solution.py:111
  190.1 3.8 %convolution_convert_fusion.1 = bf16[64,38912]{1,0:T(8,128)(2,1)} fusion(bf16[32,38912]{1,0:T(8,128)(2,1)S(1)} %bitcast.84, s32[32]{0:T(128)S(1)} %copy-done.27), kind=kOutput, calls=%fused_computation.1 | convolution fusion | flops 161875968 | bytes 7471232 | tf_op jit(solution)/shard_map/dot_general | solution.py:25
  193.9 5.0 %all-to-all-start.2 = ((bf16[8,8,19,2048]{3,1,2,0:T(8,128)(2,1)}), bf16[8,8,19,2048]{3,1,2,0:T(8,128)(2,1)}, u32[]{:S(2)}, u32[]{:S(2)}) async-start(bf16[8,8,19,2048]{3,1,2,0:T(8,128)(2,1)} %bitcast.82), calls=%async_computation.2 | async-start | bytes 9961472 | tf_op jit(solution)/shard_map/all_to_all | solution.py:181
  200.4 3.2 %multiply_reduce_fusion.3 = f32[32,2048]{1,0:T(8,128)S(1)} fusion(f32[32,16]{1,0:T(8,128)S(1)} %bitcast.90, f32[32,2048]{1,0:T(8,128)S(1)} %get-tuple-element.25, f32[16,2048]{1,0:T(8,128)S(1)} %exponential_negate_fusion, f32[32,2048]{1,0:T(8,128)S(1)} %copy-done.7, f32[32,16]{1,0:T(8,128)S(1)} %bitcast.91, bf16[32,19,2048]{2,1,0:T(8,128)(2,1)} %reshape.130), kind=kLoop, calls=%fused_computation.13 | loop fusion | flops 7274496 | bytes 3018752 | tf_op jit(solution)/shard_map/reduce_sum | solution.py:111
  205.7 50.6 %all-to-all-done.2 = bf16[8,8,19,2048]{3,1,2,0:T(8,128)(2,1)} async-done(((bf16[8,8,19,2048]{3,1,2,0:T(8,128)(2,1)}), bf16[8,8,19,2048]{3,1,2,0:T(8,128)(2,1)}, u32[]{:S(2)}, u32[]{:S(2)}) %all-to-all-start.2) | async-done | bytes 4980768 | tf_op jit(solution)/shard_map/all_to_all | solution.py:181
  256.3 6.3 %convolution_convert_fusion = bf16[64,38912]{1,0:T(8,128)(2,1)} fusion(bf16[64,38912]{1,0:T(8,128)(2,1)} %bitcast.33, s32[64]{0:T(128)S(1)} %copy-done.25), kind=kOutput, calls=%fused_computation | convolution fusion | flops 321261568 | bytes 9961728 | tf_op jit(solution)/shard_map/dot_general | solution.py:25
  262.5 8.4 %reshape.136 = bf16[64,19,2048]{2,1,0:T(8,128)(2,1)} reshape(bf16[64,38912]{1,0:T(8,128)(2,1)} %convolution_convert_fusion) | data formatting | bytes 9961472 | tf_op jit(solution)/shard_map/reshape | solution.py:26
  270.9 12.6 %copy_select_fusion = bf16[64,19,2048]{2,1,0:T(8,128)(2,1)} fusion(bf16[64,19,2048]{2,1,0:T(8,128)(2,1)} %reshape.136, bf16[64,19,2048]{2,0,1:T(8,128)(2,1)} %param.19, pred[64]{0:T(512)(128)(4,1)S(1)} %copy-done.28), kind=kLoop, calls=%fused_computation.4 | loop fusion | flops 2490368 | bytes 14942272 | tf_op jit(solution)/shard_map/jit(_where)/select_n | solution.py:33
  283.5 7.9 %copy.177 = bf16[64,19,2048]{2,0,1:T(8,128)(2,1)} copy(bf16[64,19,2048]{2,1,0:T(8,128)(2,1)} %copy_select_fusion) | data formatting | bytes 9961472
  (104 shorter events, 27.5 us)
Async XLA Ops:
  7.2 166.8 %copy-start = (bf16[512,2048]{1,0:T(8,128)(2,1)S(1)}, bf16[512,2048]{1,0:T(8,128)(2,1)}, u32[]{:S(2)}) copy-start(bf16[512,2048]{1,0:T(8,128)(2,1)} %param.30) | copy-start | bytes 6291460
  9.6 81.0 %copy-start.26 = (s32[32]{0:T(128)}, s32[32]{0:T(128)S(1)}, u32[]{:S(2)}) copy-start(s32[32]{0:T(128)S(1)} %get-tuple-element.54) | copy-start | bytes 388
  10.4 10.6 %all-to-all-start = ((s32[8,1,8]{2,1,0:T(1,128)}), s32[8,1,8]{2,1,0:T(1,128)S(1)}, u32[]{:S(2)}, u32[]{:S(2)}) async-start(s32[8,1,8]{2,1,0:T(1,128)} %bitcast.1), calls=%async_computation | async-start | bytes 8192 | tf_op jit(solution)/shard_map/all_to_all | solution.py:165
  22.3 6.1 %copy-start.23 = (s32[64]{0:T(128)}, s32[64]{0:T(128)S(1)}, u32[]{:S(2)}) copy-start(s32[64]{0:T(128)S(1)} %eq.38) | copy-start | bytes 772
  28.5 62.2 %all-to-all-start.1 = ((bf16[8,8,19,2048]{3,1,2,0:T(8,128)(2,1)}), bf16[8,8,19,2048]{3,1,2,0:T(8,128)(2,1)}, u32[]{:S(2)}, u32[]{:S(2)}) async-start(bf16[8,8,19,2048]{3,1,2,0:T(8,128)(2,1)} %bitcast.80), calls=%async_computation.1 | async-start | bytes 9961472 | tf_op jit(solution)/shard_map/all_to_all | solution.py:169
  33.1 6.6 %copy-start.29 = (s32[32]{0:T(128)S(1)}, s32[32]{0:T(128)}, u32[]{:S(2)}) copy-start(s32[32]{0:T(128)} %param.22) | copy-start | bytes 388
  33.1 6.8 %copy-start.3 = (bf16[32,4,2048]{2,1,0:T(4,128)(2,1)S(1)}, bf16[32,4,2048]{2,1,0:T(4,128)(2,1)}, u32[]{:S(2)}) copy-start(bf16[32,4,2048]{2,1,0:T(4,128)(2,1)} %param.17) | copy-start | bytes 1572868
  33.1 7.9 %copy-start.14 = (f32[4,2048]{1,0:T(4,128)S(1)}, f32[4,2048]{1,0:T(4,128)}, u32[]{:S(2)}) copy-start(f32[4,2048]{1,0:T(4,128)} %param.23) | copy-start | bytes 98308
  33.1 7.9 %copy-start.11 = (f32[16,2048]{1,0:T(8,128)S(1)}, f32[16,2048]{1,0:T(8,128)}, u32[]{:S(2)}) copy-start(f32[16,2048]{1,0:T(8,128)} %param.32) | copy-start | bytes 393220
  33.1 139.2 %all-reduce.3.cloned.1.call-start = ((), (), s32[]{:S(2)}) async-start(), calls=%async_computation.3 | async-start | bytes 524288 | tf_op jit(solution)/shard_map/psum | solution.py:81
  95.5 6.8 %copy-start.21 = (f32[2048]{0:T(1024)S(1)}, f32[2048]{0:T(1024)}, u32[]{:S(2)}) copy-start(f32[2048]{0:T(1024)} %param.24) | copy-start | bytes 24580
  101.7 7.6 %copy-start.12 = (bf16[2048,32]{0,1:T(8,128)(2,1)S(1)}, bf16[2048,32]{0,1:T(8,128)(2,1)}, u32[]{:S(2)}) copy-start(bf16[2048,32]{0,1:T(8,128)(2,1)} %param.26) | copy-start | bytes 393220
  179.5 8.4 %copy-start.6 = (f32[32,2048]{1,0:T(8,128)}, f32[32,2048]{1,0:T(8,128)S(1)}, u32[]{:S(2)}) copy-start(f32[32,2048]{1,0:T(8,128)S(1)} %get-tuple-element.34) | copy-start | bytes 786436
  179.5 8.4 %copy-start.5 = (bf16[32,3,2048]{2,1,0:T(4,128)(2,1)S(1)}, bf16[32,3,2048]{2,1,0:T(4,128)(2,1)}, u32[]{:S(2)}) copy-start(bf16[32,3,2048]{2,1,0:T(4,128)(2,1)} %slice.135) | copy-start | bytes 1179652
  193.9 5.0 %copy-start.4 = (bf16[32,4,2048]{2,1,0:T(4,128)(2,1)S(1)}, bf16[32,4,2048]{2,1,0:T(4,128)(2,1)}, u32[]{:S(2)}) copy-start(bf16[32,4,2048]{2,1,0:T(4,128)(2,1)} %param.18) | copy-start | bytes 1572868
  193.9 5.8 %copy-start.24 = (s32[64]{0:T(128)S(1)}, s32[64]{0:T(128)}, u32[]{:S(2)}) copy-start(s32[64]{0:T(128)} %copy-done.23) | copy-start | bytes 772
  193.9 6.5 %copy-start.7 = (f32[32,2048]{1,0:T(8,128)S(1)}, f32[32,2048]{1,0:T(8,128)}, u32[]{:S(2)}) copy-start(f32[32,2048]{1,0:T(8,128)} %copy-done.6) | copy-start | bytes 786436
  193.9 6.5 %copy-start.13 = (f32[32,1,16]{2,1,0:T(1,128)S(1)}, f32[32,1,16]{2,1,0:T(1,128)}, u32[]{:S(2)}) copy-start(f32[32,1,16]{2,1,0:T(1,128)} %get-tuple-element.38) | copy-start | bytes 6148
  193.9 62.3 %all-to-all-start.2 = ((bf16[8,8,19,2048]{3,1,2,0:T(8,128)(2,1)}), bf16[8,8,19,2048]{3,1,2,0:T(8,128)(2,1)}, u32[]{:S(2)}, u32[]{:S(2)}) async-start(bf16[8,8,19,2048]{3,1,2,0:T(8,128)(2,1)} %bitcast.82), calls=%async_computation.2 | async-start | bytes 9961472 | tf_op jit(solution)/shard_map/all_to_all | solution.py:181
  198.9 4.7 %copy-start.8 = (f32[32,2048]{1,0:T(8,128)S(1)}, f32[32,2048]{1,0:T(8,128)}, u32[]{:S(2)}) copy-start(f32[32,2048]{1,0:T(8,128)} %get-tuple-element.10) | copy-start | bytes 786436
  199.0 4.7 %copy-start.9 = (f32[32,2048]{1,0:T(8,128)S(1)}, f32[32,2048]{1,0:T(8,128)}, u32[]{:S(2)}) copy-start(f32[32,2048]{1,0:T(8,128)} %get-tuple-element.11) | copy-start | bytes 786436
  203.6 52.6 %copy-start.25 = (s32[64]{0:T(128)S(1)}, s32[64]{0:T(128)}, u32[]{:S(2)}) copy-start(s32[64]{0:T(128)} %copy-done.23) | copy-start | bytes 772
  262.5 8.4 %copy-start.28 = (pred[64]{0:T(512)(128)(4,1)S(1)}, pred[64]{0:T(512)(128)(4,1)}, u32[]{:S(2)}) copy-start(pred[64]{0:T(512)(128)(4,1)} %fusion.31) | copy-start | bytes 196
  270.9 20.5 %copy-start.1 = (bf16[512,2048]{1,0:T(8,128)(2,1)S(1)}, bf16[512,2048]{1,0:T(8,128)(2,1)}, u32[]{:S(2)}) copy-start(bf16[512,2048]{1,0:T(8,128)(2,1)} %param.30) | copy-start | bytes 6291460
  (10 other events, 24.0 us)
Sparse Core Ops, SparseCore 0:
  140.5 31.7 all-reduce.2
where the time goes:
time: 300 us; the launch traced here: 298 us
  waiting for transfers between devices  128 us (43%)
  local copies, waits for them, and re-layouts  53.9 us (18%)
  matrix products  36.5 us (12%)
  other arithmetic  31.3 us (10%)
  blocking collectives  19.2 us (6%)
  starting transfers between devices  14.8 us (5%)
  between operations  14.5 us (5%)
    all_to_all x1, waiting for transfers between devices, local(): lax.all_to_all(outgoing.reshape(owners, per_owner, depth_rows, chan_count...  50.6 us
    all_to_all x1, waiting for transfers between devices, local(): lax.all_to_all(picked.reshape(owners, per_owner, depth_rows, chan_count),...  49.5 us
    psum x1, waiting for transfers between devices, mixer_rows(): lax.psum((part_low, part_maps, part_adapt), 'tp')  27.9 us
    psum x1, blocking collectives, mixer_rows(): lax.psum((part_low, part_maps, part_adapt), 'tp')  19.2 us
    unnamed x65, local copies, waits for them, and re-layouts  18 us
    select_n x1, other arithmetic, write_rows(): return jnp.where(reached[:, None, None], placed, table)  12.6 us
    reduce_sum x2, other arithmetic, mixer_rows(): jnp.sum(maps_out[:, step_idx, :, None] * state_now, axis=1)  11.1 us
    dot_general x2, matrix products, take_rows(): jnp.dot(selector, flattened, preferred_element_type=jnp.float32)  11 us
  transfers between devices with their start and end apart: 4, of which 3 were waited for; matrix products, arithmetic and copies ran while one was open for 8% of the time, Pallas kernels for 0%

commit v1 on v0

--- a/solution.py
+++ b/solution.py
@@ -24,19 +24,6 @@
     selector = one_hot_rows(index_list, count)
     placed = jnp.dot(selector.T, flattened, preferred_element_type=jnp.float32).astype(values.dtype)
     return placed.reshape((count,) + values.shape[1:])
-
-
-def write_rows(table, values, index_list):
-    count = table.shape[0]
-    placed = place_rows(values, index_list, count)
-    reached = jnp.any(index_list[:, None] == jnp.arange(count, dtype=jnp.int32)[None, :], axis=0)
-    return jnp.where(reached[:, None, None], placed, table)
-
-
-def place_ints(values, index_list, count, filler):
-    matches = index_list[:, None] == jnp.arange(count, dtype=jnp.int32)[None, :]
-    summed = jnp.sum(jnp.where(matches, (values - filler)[:, None], 0), axis=0)
-    return summed + filler
 
 
 def mixer_rows(
@@ -127,67 +114,65 @@
     session_holder,
     session_slot,
     conversation_customer,
-    filter_tap_weight,
-    filter_bias,
-    lowrank_step_weight,
-    state_maps_weight,
-    adapter_down_maps,
-    adapter_up_maps,
-    step_size_gain,
-    step_up_weight,
-    step_size_bias,
-    log_decay_rates,
-    skip_factor,
+    *weights,
 ):
     owners = lax.axis_size("pool")
     slot_count, depth_rows, chan_count = slot_state_cache.shape
+    row_count, step_count, _ = projected_mixer.shape
     per_owner = slot_count // owners
-    slots_each = owners * per_owner
     owner_match = (session_holder[:, None] == jnp.arange(owners, dtype=jnp.int32)[None, :]).astype(
         jnp.int32
     )
     owner_rank = jnp.sum((jnp.cumsum(owner_match, axis=0) - 1) * owner_match, axis=1)
     target = session_holder * per_owner + owner_rank
-    request_slot = place_ints(session_slot, target, slots_each, -1)
-    weights = (
-        filter_tap_weight,
-        filter_bias,
-        lowrank_step_weight,
-        state_maps_weight,
-        adapter_down_maps,
-        adapter_up_maps,
-        step_size_gain,
-        step_up_weight,
-        step_size_bias,
-        log_decay_rates,
-        skip_factor,
-    )
-    asked_slot = lax.all_to_all(
-        request_slot.reshape(owners, per_owner), "pool", split_axis=0, concat_axis=0, tiled=True
-    ).reshape(slots_each)
-    picked = take_rows(slot_state_cache, asked_slot)
-    arrived = lax.all_to_all(
-        picked.reshape(owners, per_owner, depth_rows, chan_count),
-        "pool",
-        split_axis=0,
-        concat_axis=0,
-        tiled=True,
-    )
-    saved_state = take_rows(arrived.reshape(slots_each, depth_rows, chan_count), target)
-    gated_result, newest_state = mixer_rows(
-        projected_mixer, projected_gate, saved_state, conversation_customer, *weights
-    )
-    outgoing = place_rows(newest_state, target, slots_each)
-    came_back = lax.all_to_all(
-        outgoing.reshape(owners, per_owner, depth_rows, chan_count),
-        "pool",
-        split_axis=0,
-        concat_axis=0,
-        tiled=True,
-    )
-    new_cache = write_rows(
-        slot_state_cache, came_back.reshape(slots_each, depth_rows, chan_count), asked_slot
-    )
+
+    def exchange(values):
+        return lax.all_to_all(
+            values.reshape((owners, per_owner) + values.shape[1:]),
+            "pool",
+            split_axis=0,
+            concat_axis=0,
+            tiled=True,
+        ).reshape(values.shape)
+
+    labels = jnp.concatenate(
+        [
+            one_hot_rows(session_slot, slot_count),
+            one_hot_rows(conversation_customer, TENANT_COUNT),
+        ],
+        axis=1,
+    )
+    labels = jnp.broadcast_to(labels[:, None, :], (row_count, step_count, labels.shape[1]))
+    sent = place_rows(jnp.concatenate([projected_mixer, labels], axis=2), target, slot_count)
+    sent_gate = place_rows(projected_gate, target, slot_count)
+    arrived = exchange(sent)
+    arrived_gate = exchange(sent_gate)
+    selector = arrived[:, 0, chan_count : chan_count + slot_count]
+
+    def to_slots(values):
+        flattened = values.reshape(slot_count, -1)
+        return (
+            jnp.dot(selector.T, flattened, preferred_element_type=jnp.float32)
+            .astype(jnp.bfloat16)
+            .reshape(values.shape)
+        )
+
+    tenant_mask = to_slots(arrived[:, 0, chan_count + slot_count :])
+    tenant_list = jnp.argmax(tenant_mask, axis=1).astype(jnp.int32)
+    reached = jnp.sum(selector, axis=0) > 0
+    gated_slots, newest_state = mixer_rows(
+        to_slots(arrived[:, :, :chan_count]),
+        to_slots(arrived_gate),
+        slot_state_cache,
+        tenant_list,
+        *weights,
+    )
+    new_cache = jnp.where(reached[:, None, None], newest_state, slot_state_cache)
+    returned = jnp.dot(
+        selector, gated_slots.reshape(slot_count, -1), preferred_element_type=jnp.float32
+    ).astype(jnp.bfloat16)
+    came_back = exchange(returned.reshape(gated_slots.shape))
+    gated_result = take_rows(came_back, target)
     return (gated_result, new_cache)
 
 

time: 300 us -> 185 us (0.62)
  waiting for transfers between devices: 128 us -> 37.5 us
  local copies, waits for them, and re-layouts: 53.9 us -> 39.5 us
  matrix products: 36.5 us -> 27.7 us
    all_to_all x3, waiting for transfers between devices: 100 us -> 15 us  [exchange(): lax.all_to_all(values.reshape((owners, per_owner) + values.shape[1:]), 'p...]
    reshape x2 -> x4, local copies, waits for them, and re-layouts: 13.8 us -> 3.58 us  [the longest x3 3.51 us: to_slots(): return jnp.dot(selector.T, flattened, preferred_element_type=jnp.float32)...]
    dot_general x2 -> x1, matrix products: 11 us -> 1.15 us  [take_rows(): jnp.dot(selector, flattened, preferred_element_type=jnp.float32)]
    unnamed x65 -> x52, local copies, waits for them, and re-layouts: 18 us -> 10.1 us
    dot_general x2, matrix products: 10.1 us -> 3.1 us  [place_rows(): jnp.dot(selector.T, flattened, preferred_element_type=jnp.float32)]
    dot_general x0 -> x4, matrix products: none -> 6.09 us  [the longest x3 3.95 us: to_slots(): jnp.dot(selector.T, flattened, preferred_element_type=jnp.float32)]
    select_n x1, other arithmetic: 12.6 us -> 7.02 us  [local(): jnp.where(reached[:, None, None], newest_state, slot_state_cache)]
    psum x1, waiting for transfers between devices: 27.9 us -> 22.5 us  [mixer_rows(): lax.psum((part_low, part_maps, part_adapt), 'tp')]
  transfers between devices with their start and end apart: 4 -> 4, of which waited for: 3 -> 3; matrix products, arithmetic and copies ran while one was open for 8% -> 30% of each run, Pallas kernels for 0% -> 0%
where the time goes in v1:
time: 185 us; the launch traced here: 184 us
  local copies, waits for them, and re-layouts  39.5 us (21%)
  waiting for transfers between devices  37.5 us (20%)
  other arithmetic  32.2 us (17%)
  matrix products  27.7 us (15%)
  blocking collectives  19.7 us (11%)
  between operations  14.5 us (8%)
  starting transfers between devices  13.1 us (7%)
    psum x1, waiting for transfers between devices, mixer_rows(): lax.psum((part_low, part_maps, part_adapt), 'tp')  22.5 us
    psum x1, blocking collectives, mixer_rows(): lax.psum((part_low, part_maps, part_adapt), 'tp')  19.7 us
    reduce_sum x2, other arithmetic, mixer_rows(): jnp.sum(maps_out[:, step_idx, :, None] * state_now, axis=1)  15.8 us
    all_to_all x3, waiting for transfers between devices, exchange(): lax.all_to_all(values.reshape((owners, per_owner) + values.shape[1:]), 'p...  15 us
    all_to_all x3, starting transfers between devices, exchange(): lax.all_to_all(values.reshape((owners, per_owner) + values.shape[1:]), 'p...  13.1 us
    unnamed x52, local copies, waits for them, and re-layouts  10.1 us
    dot_general x1, matrix products, mixer_rows(): jnp.dot(flattened_rows, adapter_down_maps, preferred_element_type=jnp.flo...  7.27 us
    select_n x1, other arithmetic, local(): jnp.where(reached[:, None, None], newest_state, slot_state_cache)  7.02 us
  transfers between devices with their start and end apart: 4, of which 3 were waited for; matrix products, arithmetic and copies ran while one was open for 30% of the time, Pallas kernels for 0%

profile of v1, /device:TPU:0, one launch (start us, length us, event | category | flops | bytes accessed | tf_op | source)
XLA Modules:
  0.0 184.2 jit_solution(12999240779720748782)
XLA Ops:
  11.5 5.2 %all-to-all-start = ((bf16[8,8,4,2176]{3,1,2,0:T(8,128)(2,1)}), bf16[8,8,4,2176]{3,1,2,0:T(8,128)(2,1)S(1)}, u32[]{:S(2)}, u32[]{:S(2)}) async-start(bf16[8,8,4,2176]{3,1,2,0:T(8,128)(2,1)} %bitcast.115), calls=%async_computation | async-start | bytes 2228224 | tf_op jit(solution)/shard_map/all_to_all | solution.py:130
  19.5 6.5 %copy.94 = bf16[2048,1024]{0,1:T(8,128)(2,1)} copy(bf16[2048,1024]{1,0:T(8,128)(2,1)} %param.27) | data formatting | bytes 8388608 | tf_op args[10]
  26.1 6.7 %all-to-all-done = bf16[8,8,4,2176]{3,1,2,0:T(8,128)(2,1)S(1)} async-done(((bf16[8,8,4,2176]{3,1,2,0:T(8,128)(2,1)}), bf16[8,8,4,2176]{3,1,2,0:T(8,128)(2,1)S(1)}, u32[]{:S(2)}, u32[]{:S(2)}) %all-to-all-start) | async-done | bytes 1114144 | tf_op jit(solution)/shard_map/all_to_all | solution.py:130
  32.8 4.2 %all-to-all-start.1 = ((bf16[8,8,4,2048]{3,1,2,0:T(8,128)(2,1)}), bf16[8,8,4,2048]{3,1,2,0:T(8,128)(2,1)}, u32[]{:S(2)}, u32[]{:S(2)}) async-start(bf16[8,8,4,2048]{3,1,2,0:T(8,128)(2,1)} %bitcast.118), calls=%async_computation.1 | async-start | bytes 2097152 | tf_op jit(solution)/shard_map/all_to_all | solution.py:130
  39.8 2.3 %fusion.46 = (f32[64,4,2048]{2,0,1:T(8,128)}, bf16[64,4,2048]{2,0,1:T(8,128)(2,1)S(1)}) fusion(bf16[64,4,2048]{2,0,1:T(8,128)(2,1)S(1)} %bitcast.116, f32[2048]{0:T(1024)S(1)} %bitcast.134, bf16[64,3,2048]{2,0,1:T(8,128)(2,1)S(1)} %slice-done.2, f32[2048]{0:T(1024)S(1)} %bitcast.135, f32[2048]{0:T(1024)S(1)} %bitcast.133, f32[2048]{0:T(1024)S(1)} %bitcast.132, ...), kind=kLoop, calls=%fused_computation.108 | loop fusion | flops 11010048 | bytes 5021696 | tf_op jit(solution)/shard_map/convert_element_type | solution.py:88
  47.1 3.4 %fusion.54 = f32[256,512]{1,0:T(8,128)} fusion(bf16[256,2048]{1,0:T(8,128)(2,1)} %reshape.137, bf16[2048,512]{1,0:T(8,128)(2,1)} %param.25), kind=kOutput, calls=%fused_computation.116 | convolution fusion | flops 536870912 | bytes 3670016 | tf_op jit(solution)/shard_map/dot_general | solution.py:57
  50.5 7.3 %fusion.6 = f32[256,16]{0,1:T(8,128)S(1)} fusion(bf16[256,2048,1]{1,0,2:T(8,128)(2,1)} %reshape.144, bf16[64,16,2048]{2,1,0:T(8,128)(2,1)} %bitcast.117, pred[256,64]{0,1:T(8,128)(4,1)S(1)} %iota_compare_fusion), kind=kOutput, calls=%fused_computation.27 | convolution fusion | flops 1074262016 | bytes 5275648 | tf_op jit(solution)/shard_map/dot_general | solution.py:59
  57.8 19.7 %all-reduce = (f32[256,32]{0,1:T(8,128)S(1)}, bf16[256,16]{0,1:T(8,128)(2,1)S(1)}) all-reduce(f32[256,32]{0,1:T(8,128)S(1)} %fusion.53, f32[256,16]{0,1:T(8,128)S(1)} %fusion.6), channel_id=1, replica_groups=mesh['pool'=8,'tp'=4] {'tp'}, use_global_device_ids=true, to_apply=%region_2.3 | all-reduce | flops 12288 | bytes 90112 | tf_op jit(solution)/shard_map/psum | solution.py:68
  79.9 2.2 %copy.96 = bf16[256,64,16]{0,2,1:T(8,128)(2,1)} copy(bf16[256,64,16]{0,1,2:T(8,128)(2,1)} %select_convert_fusion) | data formatting | bytes 1048576 | tf_op jit(solution)/shard_map/convert_element_type | solution.py:72
  89.5 2.7 %convolution_convert_fusion.2 = bf16[64,8192]{1,0:T(8,128)(2,1)} fusion(bf16[64,8192]{1,0:T(8,128)(2,1)} %bitcast.19, bf16[64,4,2176]{2,0,1:T(8,128)(2,1)} %bitcast.113), kind=kOutput, calls=%fused_computation.2 | convolution fusion | flops 67633152 | bytes 2113536 | tf_op jit(solution)/shard_map/dot_general | solution.py:155
  92.2 1.8 %reshape.142 = bf16[64,4,2048]{2,1,0:T(4,128)(2,1)S(1)} reshape(bf16[64,8192]{1,0:T(8,128)(2,1)} %convolution_convert_fusion.2) | data formatting | bytes 2097152 | tf_op jit(solution)/shard_map/reshape | solution.py:157
  94.1 2.6 %fusion.48 = (bf16[64,1,2048]{2,1,0:T(2,128)(2,1)}, bf16[64,1,2048]{2,1,0:T(2,128)(2,1)}, bf16[64,1,2048]{2,1,0:T(2,128)(2,1)}, bf16[64,1,2048]{2,1,0:T(2,128)(2,1)}) fusion(bf16[64,4,2048]{2,1,0:T(4,128)(2,1)S(1)} %reshape.142), kind=kLoop, calls=%fused_computation.110 | loop fusion | bytes 2097152 | tf_op jit(solution)/shard_map/slice | solution.py:101
  96.7 22.5 %all-reduce.3.cloned.1.call-done = f32[256,512]{1,0:T(8,128)} async-done(((f32[256,512]{1,0:T(8,128)}), f32[256,512]{1,0:T(8,128)}) %all-reduce.3.cloned.1.call-update) | async-done | bytes 524304 | tf_op jit(solution)/shard_map/psum | solution.py:68
  119.2 2.1 %multiply_reduce_fusion.4 = (f32[256]{0:T(256)S(1)}, f32[256,512]{1,0:T(8,128)S(1)}) fusion(f32[256,512]{1,0:T(8,128)} %all-reduce.3.cloned.1.call-done, bf16[256,1024]{0,1:T(8,128)(2,1)} %bitcast.124, bf16[1024,512]{1,0:T(8,128)(2,1)} %param.28), kind=kOutput, calls=%fused_computation.72 | convolution fusion | flops 268828416 | bytes 2622464 | tf_op jit(solution)/shard_map/dot_general | solution.py:74
  121.3 3.0 %compare_select_fusion = f32[256,2048]{1,0:T(8,128)} fusion(bf16[512,2048]{1,0:T(8,128)(2,1)S(1)} %copy-done, f32[2048]{0:T(1024)S(1)} %copy-done.20, f32[256,512]{1,0:T(8,128)S(1)} %get-tuple-element.47, f32[512]{0:T(512)S(1)} %copy-done.21, f32[256]{0:T(256)S(1)} %add_sqrt_fusion), kind=kOutput, calls=%fused_computation.14 | convolution fusion | flops 540934144 | bytes 4729856 | tf_op jit(solution)/shard_map/dot_general | solution.py:81
  124.2 2.8 %reshape.139 = f32[64,4,2048]{2,1,0:T(4,128)} reshape(f32[256,2048]{1,0:T(8,128)} %compare_select_fusion) | data formatting | bytes 4194304 | tf_op jit(solution)/shard_map/reshape | solution.py:84
  127.0 5.9 %fusion.47 = (f32[64,1,2048]{2,1,0:T(1,128)S(1)}, f32[64,1,2048]{2,1,0:T(1,128)S(1)}, f32[64,1,2048]{2,1,0:T(1,128)S(1)}, f32[64,1,2048]{2,1,0:T(1,128)S(1)}) fusion(f32[64,4,2048]{2,1,0:T(4,128)} %reshape.139), kind=kLoop, calls=%fused_computation.109 | loop fusion | bytes 4194304 | tf_op jit(solution)/shard_map/slice | solution.py:92
  135.1 3.1 %multiply_reduce_fusion.3 = f32[64,2048]{1,0:T(8,128)S(1)} fusion(f32[64,16]{0,1:T(8,128)S(1)} %bitcast.129, f32[64,2048]{1,0:T(8,128)S(1)} %get-tuple-element.19, f32[16,2048]{1,0:T(8,128)S(1)} %exponential_negate_fusion, f32[64,2048]{1,0:T(8,128)S(1)} %get-tuple-element.28, f32[64,16]{0,1:T(8,128)S(1)} %bitcast.131, bf16[64,19,2048]{2,0,1:T(8,128)(2,1)S(1)} %bitcast.107), kind=kLoop, calls=%fused_computation.12 | loop fusion | flops 14548992 | bytes 5906432 | tf_op jit(solution)/shard_map/reduce_sum | solution.py:98
  138.3 12.7 %multiply_reduce_fusion.1 = (f32[64,2048]{1,0:T(8,128)S(1)}, f32[64,2048]{1,0:T(8,128)S(1)}, f32[64,2048]{1,0:T(8,128)S(1)}, bf16[64,16,2048]{2,0,1:T(8,128)(2,1)}) fusion(f32[64,16]{0,1:T(8,128)S(1)} %bitcast.139, f32[64,2048]{1,0:T(8,128)S(1)} %get-tuple-element.17, f32[64,2048]{1,0:T(8,128)S(1)} %get-tuple-element.30, f32[64,16]{0,1:T(8,128)S(1)} %bitcast.138, ...), kind=kLoop, calls=%fused_computation.8 | loop fusion | flops 49938432 | bytes 14315520 | tf_op jit(solution)/shard_map/reduce_sum | solution.py:98
  152.8 2.1 %convolution_convert_fusion.1 = bf16[64,8192]{1,0:T(8,128)(2,1)} fusion(bf16[64,8192]{1,0:T(8,128)(2,1)S(1)} %bitcast.120, bf16[64,4,2176]{2,0,1:T(8,128)(2,1)} %bitcast.114), kind=kOutput, calls=%fused_computation.1 | convolution fusion | flops 67633152 | bytes 2113536 | tf_op jit(solution)/shard_map/dot_general | solution.py:171
  154.9 3.7 %all-to-all-start.2 = ((bf16[8,8,4,2048]{3,1,2,0:T(8,128)(2,1)}), bf16[8,8,4,2048]{3,1,2,0:T(8,128)(2,1)S(1)}, u32[]{:S(2)}, u32[]{:S(2)}) async-start(bf16[8,8,4,2048]{3,1,2,0:T(8,128)(2,1)} %bitcast.35), calls=%async_computation.2 | async-start | bytes 2097152 | tf_op jit(solution)/shard_map/all_to_all | solution.py:130
  158.6 7.0 %maximum_select_fusion = bf16[64,19,2048]{2,0,1:T(8,128)(2,1)} fusion(bf16[64,19,2048]{2,0,1:T(8,128)(2,1)} %param.19, bf16[64,3,2048]{2,0,1:T(8,128)(2,1)} %copy.114, bf16[64,16,2048]{2,0,1:T(8,128)(2,1)} %get-tuple-element.11, pred[64]{0:T(512)(128)(4,1)S(1)} %broadcast_compare_fusion), kind=kLoop, calls=%fused_computation.15 | loop fusion | flops 4980736 | bytes 14942272 | tf_op jit(solution)/shard_map/jit(_where)/select_n | solution.py:170
  165.7 8.4 %all-to-all-done.2 = bf16[8,8,4,2048]{3,1,2,0:T(8,128)(2,1)S(1)} async-done(((bf16[8,8,4,2048]{3,1,2,0:T(8,128)(2,1)}), bf16[8,8,4,2048]{3,1,2,0:T(8,128)(2,1)S(1)}, u32[]{:S(2)}, u32[]{:S(2)}) %all-to-all-start.2) | async-done | bytes 1048608 | tf_op jit(solution)/shard_map/all_to_all | solution.py:130
  175.2 2.2 %reshape.143 = bf16[32,4,2048]{2,1,0:T(4,128)(2,1)} reshape(bf16[32,8192]{1,0:T(8,128)(2,1)} %convolution_convert_fusion.5) | data formatting | bytes 1048576 | tf_op jit(solution)/shard_map/reshape | solution.py:19
  (106 shorter events, 29.7 us)
Async XLA Ops:
  7.2 114.1 %copy-start = (bf16[512,2048]{1,0:T(8,128)(2,1)S(1)}, bf16[512,2048]{1,0:T(8,128)(2,1)}, u32[]{:S(2)}) copy-start(bf16[512,2048]{1,0:T(8,128)(2,1)} %param.30) | copy-start | bytes 6291460
  7.2 2.4 %copy-start.19 = (s32[32]{0:T(128)S(1)}, s32[32]{0:T(128)}, u32[]{:S(2)}) copy-start(s32[32]{0:T(128)} %param.20) | copy-start | bytes 388
  9.9 8.1 %copy-start.17 = (s32[32]{0:T(128)}, s32[32]{0:T(128)S(1)}, u32[]{:S(2)}) copy-start(s32[32]{0:T(128)S(1)} %multiply_add_fusion.4) | copy-start | bytes 388
  11.5 21.3 %all-to-all-start = ((bf16[8,8,4,2176]{3,1,2,0:T(8,128)(2,1)}), bf16[8,8,4,2176]{3,1,2,0:T(8,128)(2,1)S(1)}, u32[]{:S(2)}, u32[]{:S(2)}) async-start(bf16[8,8,4,2176]{3,1,2,0:T(8,128)(2,1)} %bitcast.115), calls=%async_computation | async-start | bytes 2228224 | tf_op jit(solution)/shard_map/all_to_all | solution.py:130
  19.5 6.5 %copy-start.14 = (f32[4,2048]{1,0:T(4,128)S(1)}, f32[4,2048]{1,0:T(4,128)}, u32[]{:S(2)}) copy-start(f32[4,2048]{1,0:T(4,128)} %param.23) | copy-start | bytes 98308
  19.5 6.5 %copy-start.12 = (f32[16,2048]{1,0:T(8,128)S(1)}, f32[16,2048]{1,0:T(8,128)}, u32[]{:S(2)}) copy-start(f32[16,2048]{1,0:T(8,128)} %param.32) | copy-start | bytes 393220
  32.8 56.8 %all-to-all-start.1 = ((bf16[8,8,4,2048]{3,1,2,0:T(8,128)(2,1)}), bf16[8,8,4,2048]{3,1,2,0:T(8,128)(2,1)}, u32[]{:S(2)}, u32[]{:S(2)}) async-start(bf16[8,8,4,2048]{3,1,2,0:T(8,128)(2,1)} %bitcast.118), calls=%async_computation.1 | async-start | bytes 2097152 | tf_op jit(solution)/shard_map/all_to_all | solution.py:130
  37.0 82.2 %all-reduce.3.cloned.1.call-start = ((), (), s32[]{:S(2)}) async-start(), calls=%async_computation.3 | async-start | bytes 1048576 | tf_op jit(solution)/shard_map/psum | solution.py:68
  42.9 2.5 %copy-start.11 = (bf16[2048,32]{0,1:T(8,128)(2,1)S(1)}, bf16[2048,32]{0,1:T(8,128)(2,1)}, u32[]{:S(2)}) copy-start(bf16[2048,32]{0,1:T(8,128)(2,1)} %param.26) | copy-start | bytes 393220
  50.5 27.9 %copy-start.4 = (bf16[64,8192]{1,0:T(8,128)(2,1)S(1)}, bf16[64,8192]{1,0:T(8,128)(2,1)}, u32[]{:S(2)}) copy-start(bf16[64,8192]{1,0:T(8,128)(2,1)} %copy-done.3) | copy-start | bytes 3145732
  79.9 6.7 %copy-start.6 = (bf16[64,4,2048]{2,1,0:T(4,128)(2,1)S(1)}, bf16[64,4,2048]{2,1,0:T(4,128)(2,1)}, u32[]{:S(2)}) copy-start(bf16[64,4,2048]{2,1,0:T(4,128)(2,1)} %reshape.136) | copy-start | bytes 3145732
  96.7 24.6 %copy-start.20 = (f32[2048]{0:T(1024)S(1)}, f32[2048]{0:T(1024)}, u32[]{:S(2)}) copy-start(f32[2048]{0:T(1024)} %param.31) | copy-start | bytes 24580
  96.7 24.6 %copy-start.21 = (f32[512]{0:T(512)S(1)}, f32[512]{0:T(512)}, u32[]{:S(2)}) copy-start(f32[512]{0:T(512)} %param.29) | copy-start | bytes 6148
  127.0 5.9 %copy-start.2 = (f32[64,4,2048]{2,0,1:T(8,128)S(1)}, f32[64,4,2048]{2,0,1:T(8,128)}, u32[]{:S(2)}) copy-start(f32[64,4,2048]{2,0,1:T(8,128)} %get-tuple-element.9) | copy-start | bytes 6291460
  127.0 7.1 %slice-start = ((s8[4980736]{0:T(1024)(128)(4,1)}), s8[786432]{0:T(1024)(128)(4,1)S(1)}, s32[]{:S(2)}) async-start(s8[4980736]{0:T(1024)(128)(4,1)} %bitcast.106), calls=%async_computation.4 | async-start | bytes 1572864
  132.9 2.2 %slice-start.1 = ((s8[4980736]{0:T(1024)(128)(4,1)}), s8[4194304]{0:T(1024)(128)(4,1)S(1)}, s32[]{:S(2)}) async-start(s8[4980736]{0:T(1024)(128)(4,1)} %bitcast.106), calls=%async_computation.5 | async-start | bytes 8388608
  138.3 12.7 %copy-start.7 = (bf16[64,1,2048]{2,1,0:T(2,128)(2,1)S(1)}, bf16[64,1,2048]{2,1,0:T(2,128)(2,1)}, u32[]{:S(2)}) copy-start(bf16[64,1,2048]{2,1,0:T(2,128)(2,1)} %get-tuple-element.24) | copy-start | bytes 786436
  138.3 12.7 %copy-start.8 = (bf16[64,1,2048]{2,1,0:T(2,128)(2,1)S(1)}, bf16[64,1,2048]{2,1,0:T(2,128)(2,1)}, u32[]{:S(2)}) copy-start(bf16[64,1,2048]{2,1,0:T(2,128)(2,1)} %get-tuple-element.25) | copy-start | bytes 786436
  138.3 12.7 %copy-start.9 = (bf16[64,1,2048]{2,1,0:T(2,128)(2,1)S(1)}, bf16[64,1,2048]{2,1,0:T(2,128)(2,1)}, u32[]{:S(2)}) copy-start(bf16[64,1,2048]{2,1,0:T(2,128)(2,1)} %get-tuple-element.26) | copy-start | bytes 786436
  138.3 12.7 %copy-start.10 = (bf16[64,1,2048]{2,1,0:T(2,128)(2,1)S(1)}, bf16[64,1,2048]{2,1,0:T(2,128)(2,1)}, u32[]{:S(2)}) copy-start(bf16[64,1,2048]{2,1,0:T(2,128)(2,1)} %get-tuple-element.27) | copy-start | bytes 786436
  138.3 12.7 %copy-start.16 = (f32[2048]{0:T(1024)S(1)}, f32[2048]{0:T(1024)}, u32[]{:S(2)}) copy-start(f32[2048]{0:T(1024)} %param.33) | copy-start | bytes 24580
  154.9 19.1 %all-to-all-start.2 = ((bf16[8,8,4,2048]{3,1,2,0:T(8,128)(2,1)}), bf16[8,8,4,2048]{3,1,2,0:T(8,128)(2,1)S(1)}, u32[]{:S(2)}, u32[]{:S(2)}) async-start(bf16[8,8,4,2048]{3,1,2,0:T(8,128)(2,1)} %bitcast.35), calls=%async_computation.2 | async-start | bytes 2097152 | tf_op jit(solution)/shard_map/all_to_all | solution.py:130
  158.6 15.4 %copy-start.18 = (s32[32]{0:T(128)S(1)}, s32[32]{0:T(128)}, u32[]{:S(2)}) copy-start(s32[32]{0:T(128)} %copy-done.17) | copy-start | bytes 388
  158.6 18.8 %copy-start.1 = (bf16[512,2048]{1,0:T(8,128)(2,1)S(1)}, bf16[512,2048]{1,0:T(8,128)(2,1)}, u32[]{:S(2)}) copy-start(bf16[512,2048]{1,0:T(8,128)(2,1)} %param.30) | copy-start | bytes 6291460
  (5 other events, 8.0 us)
Sparse Core Ops, SparseCore 0:
  82.3 36.8 all-reduce.2

commit v2 on v0

v2 whole, which is shorter than its diff:
```python
import functools

import jax
import jax.numpy as jnp
from jax import lax
from jax.experimental import pallas as pl
from jax.experimental.pallas import tpu as pltpu
from jax.sharding import PartitionSpec as P

STATE = 16
ADAPTER_RANK = 16
TENANT_COUNT = 64
LABELS = 128
VMEM_BYTES = 50 * 1024 * 1024
F32 = jnp.float32
BF16 = jnp.bfloat16


def iota(shape, dim):
    return lax.broadcasted_iota(jnp.int32, shape, dim)


def as_bf16(mask):
    return jnp.where(mask, 1.0, 0.0).astype(BF16)


def whole_vmem():
    return pl.BlockSpec(memory_space=pltpu.VMEM)


def whole_any():
    return pl.BlockSpec(memory_space=pl.ANY)


def fixed(shape):
    return pl.BlockSpec(shape, lambda c: (0,) * len(shape))


def dispatch_matrix(holder, owners, per_owner, steps):
    lanes = holder.shape[1]
    named = jnp.where(iota((owners, lanes), 0) == holder, 1.0, 0.0)
    earlier = as_bf16(
        (iota((lanes, lanes), 0) // steps < iota((lanes, lanes), 1) // steps)
        & (iota((lanes, lanes), 0) % steps == 0)
    )
    before = jnp.dot(named.astype(BF16), earlier, preferred_element_type=F32)
    rank = jnp.sum(named * before, axis=0, keepdims=True)
    target = holder.astype(F32) * per_owner + rank
    shape = (owners * per_owner * steps, lanes)
    return jnp.where(
        ((iota(shape, 0) // steps).astype(F32) == target)
        & (iota(shape, 0) % steps == iota(shape, 1) % steps),
        1.0,
        0.0,
    )


def greet(pool_count, tp_count):
    barrier = pltpu.get_barrier_semaphore()
    me, mine = lax.axis_index("pool"), lax.axis_index("tp")
    for k in range(1, pool_count):
        pl.semaphore_signal(
            barrier,
            inc=1,
            device_id={"pool": lax.rem(me + k, pool_count)},
            device_id_type=pl.DeviceIdType.MESH,
        )
    for k in range(1, tp_count):
        pl.semaphore_signal(
            barrier,
            inc=1,
            device_id={"tp": lax.rem(mine + k, tp_count)},
            device_id_type=pl.DeviceIdType.MESH,
        )
    pl.semaphore_wait(barrier, max(pool_count - 1, 0) + max(tp_count - 1, 0))


def spread(source, landing, send_sem, recv_sem, local_sem, axis, count):
    me = lax.axis_index(axis)
    copies = []
    for k in range(1, count):
        there = lax.rem(me + k, count)
        copy = pltpu.make_async_remote_copy(
            src_ref=source.at[there],
            dst_ref=landing.at[me],
            send_sem=send_sem.at[k],
            recv_sem=recv_sem.at[k],
            device_id={axis: there},
            device_id_type=pl.DeviceIdType.MESH,
        )
        copy.start()
        copies.append(copy)
    own = pltpu.make_async_copy(source.at[me], landing.at[me], local_sem)
    own.start()
    copies.append(own)
    return copies


def pick_rows(selector, rows_ref, out_ref, offset=0):
    owners, block, _ = out_ref.shape
    for at in range(0, rows_ref.shape[1], 512):
        wide = min(512, rows_ref.shape[1] - at)
        part = jnp.dot(selector, rows_ref[:, at : at + wide], preferred_element_type=F32)
        out_ref[:, :, at : at + wide] = part.reshape(owners, block, wide).astype(BF16)


def send_rows(
    owners,
    per_owner,
    steps,
    holder_ref,
    slot_ref,
    tenant_ref,
    rows_ref,
    arrived_ref,
    back_ref,
    outgoing,
    send_sem,
    recv_sem,
    local_sem,
):
    picked = dispatch_matrix(holder_ref[...], owners, per_owner, steps)
    selector = picked.astype(BF16)
    back_ref[...] = picked.T.astype(BF16)
    lanes = rows_ref.shape[0]
    chans = rows_ref.shape[1]
    slots = owners * per_owner
    column = iota((lanes, LABELS), 1)
    labels = as_bf16((column == slot_ref[...]) | (column == tenant_ref[...] + slots))
    marked = jnp.dot(selector, labels, preferred_element_type=F32)
    outgoing[:, :, chans:] = marked.reshape(owners, per_owner * steps, LABELS).astype(BF16)
    pick_rows(selector, rows_ref, outgoing)
    greet(owners, 1)
    for copy in spread(outgoing, arrived_ref, send_sem, recv_sem, local_sem, "pool", owners):
        copy.wait()


def project(
    steps,
    tp_count,
    arrived_ref,
    label_ref,
    conv_ref,
    tap_ref,
    bias_ref,
    low_ref,
    maps_ref,
    down_ref,
    part_ref,
    slots_ref,
    act_ref,
    to_arrival_ref,
    to_slot_ref,
    mask_ref,
    low_acc,
    maps_acc,
    down_acc,
):
    chunk = pl.program_id(0)
    slots = conv_ref.shape[1]
    total = slots * steps
    wide = act_ref.shape[1]

    @pl.when(chunk == 0)
    def _():
        labels = label_ref[...].astype(F32).reshape(total, LABELS)
        lane = iota((LABELS, total), 0)
        expand = as_bf16(lane == iota((LABELS, total), 1) % slots)
        selected = jnp.dot(labels.astype(BF16), expand, preferred_element_type=F32)
        selected = jnp.where(
            iota((total, total), 0) % steps == iota((total, total), 1) // slots, selected, 0.0
        )
        to_arrival_ref[...] = selected.astype(BF16)
        turned = selected.T.astype(BF16)
        to_slot_ref[...] = turned
        mask_ref[...] = jnp.dot(
            turned, labels.astype(BF16), preferred_element_type=F32
        ).astype(BF16)
        low_acc[...] = jnp.zeros_like(low_acc)
        maps_acc[...] = jnp.zeros_like(maps_acc)
        down_acc[...] = jnp.zeros_like(down_acc)

    rows = arrived_ref[...].astype(F32).reshape(total, wide).astype(BF16)
    mixed = jnp.dot(to_slot_ref[...], rows, preferred_element_type=F32)
    slots_ref[...] = mixed.astype(BF16)
    window = [conv_ref[k].astype(F32) for k in range(conv_ref.shape[0])]
    window += [mixed[s * slots : (s + 1) * slots] for s in range(steps)]
    for s in range(steps):
        summed = jnp.broadcast_to(bias_ref[...], (slots, wide))
        for k in range(tap_ref.shape[0]):
            summed = summed + tap_ref[k : k + 1, :] * window[s + k]
        act_ref[s * slots : (s + 1) * slots, :] = (summed / (1.0 + jnp.exp(-summed))).astype(BF16)
    act = act_ref[...]
    low_acc[...] += jnp.dot(act, low_ref[...], preferred_element_type=F32)
    maps_acc[...] += jnp.dot(act, maps_ref[...], preferred_element_type=F32)
    down_acc[...] += jnp.dot(act, down_ref[...], preferred_element_type=F32)

    @pl.when(chunk == pl.num_programs(0) - 1)
    def _():
        ranks = down_acc.shape[1]
        column = iota((LABELS, ranks), 1) // ADAPTER_RANK
        keep = jnp.dot(
            mask_ref[...],
            as_bf16(iota((LABELS, ranks), 0) == column + slots),
            preferred_element_type=F32,
        )
        chosen = down_acc[...] * keep
        folded = chosen[:, :LABELS]
        for at in range(LABELS, ranks, LABELS):
            folded = folded + chosen[:, at : at + LABELS]
        fold = as_bf16(
            iota((LABELS, LABELS), 1)
            == iota((LABELS, LABELS), 0) % ADAPTER_RANK + 2 * STATE
        )
        tail = maps_acc[...] + jnp.dot(folded.astype(BF16), fold, preferred_element_type=F32)
        rank = low_acc.shape[1]
        part_ref[:, :, :rank] = (
            low_acc[...].reshape(tp_count, total // tp_count, rank).astype(BF16)
        )
        part_ref[:, :, rank:] = tail.reshape(tp_count, total // tp_count, LABELS).astype(BF16)


def join(
    owners,
    per_owner,
    steps,
    tp_count,
    holder_ref,
    gate_ref,
    part_ref,
    mask_ref,
    up_ref,
    gain_ref,
    arrived_ref,
    normed_ref,
    tail_ref,
    outgoing,
    landed,
    normed_own,
    tail_own,
    gate_send,
    gate_recv,
    gate_local,
    part_send,
    part_recv,
    normed_send,
    normed_recv,
    tail_send,
    tail_recv,
    own_sem,
):
    mine = lax.axis_index("tp")
    greet(owners, tp_count)
    first = []
    for k in range(1, tp_count):
        there = lax.rem(mine + k, tp_count)
        copy = pltpu.make_async_remote_copy(
            src_ref=part_ref.at[there],
            dst_ref=landed.at[k - 1],
            send_sem=part_send.at[k],
            recv_sem=part_recv.at[k],
            device_id={"tp": there},
            device_id_type=pl.DeviceIdType.MESH,
        )
        copy.start()
        first.append(copy)
    selector = dispatch_matrix(holder_ref[...], owners, per_owner, steps).astype(BF16)
    pick_rows(selector, gate_ref, outgoing)
    gates = spread(outgoing, arrived_ref, gate_send, gate_recv, gate_local, "pool", owners)
    summed = part_ref[mine].astype(F32)
    for k in range(1, tp_count):
        first[k - 1].wait()
        summed = summed + landed[k - 1].astype(F32)
    rank = gain_ref.shape[1]
    low, tail = summed[:, :rank], summed[:, rank:]
    ranks = up_ref.shape[0]
    slots = owners * per_owner
    column = iota((LABELS, ranks), 1)
    lane = iota((LABELS, ranks), 0)
    repeated = jnp.dot(
        tail.astype(BF16),
        as_bf16(lane == column % ADAPTER_RANK + 2 * STATE),
        preferred_element_type=F32,
    )
    keep = jnp.dot(
        mask_ref[mine],
        as_bf16(lane == column // ADAPTER_RANK + slots),
        preferred_element_type=F32,
    )
    middle = (repeated * keep).astype(BF16)
    pre = low + jnp.dot(middle, up_ref[...], preferred_element_type=F32)
    mean_sq = jnp.mean(pre * pre, axis=1, keepdims=True)
    normed_own[...] = (pre / jnp.sqrt(mean_sq + 1e-06) * gain_ref[...]).astype(BF16)
    tail_own[...] = tail
    last = []
    for number, (own, landing, send_sem, recv_sem) in enumerate(
        (
            (normed_own, normed_ref, normed_send, normed_recv),
            (tail_own, tail_ref, tail_send, tail_recv),
        )
    ):
        for k in range(1, tp_count):
            copy = pltpu.make_async_remote_copy(
                src_ref=own,
                dst_ref=landing.at[mine],
                send_sem=send_sem.at[k],
                recv_sem=recv_sem.at[k],
                device_id={"tp": lax.rem(mine + k, tp_count)},
                device_id_type=pl.DeviceIdType.MESH,
            )
            copy.start()
            last.append(copy)
        kept = pltpu.make_async_copy(own, landing.at[mine], own_sem.at[number])
        kept.start()
        last.append(kept)
    for copy in last + gates:
        copy.wait()


def scan(
    steps,
    normed_ref,
    tail_ref,
    up_ref,
    bias_ref,
    rate_ref,
    skip_ref,
    act_ref,
    slots_ref,
    gate_ref,
    to_arrival_ref,
    to_slot_ref,
    cache_ref,
    new_ref,
    out_ref,
    maps,
    delta,
    driven,
    newest,
    result,
    reached,
    decay,
):
    slots = cache_ref.shape[0]
    total = slots * steps
    wide = act_ref.shape[1]

    @pl.when(pl.program_id(0) == 0)
    def _():
        turned = tail_ref[...].T
        for at in range(total):
            maps[at] = jnp.broadcast_to(turned[: 2 * STATE, at : at + 1], (2 * STATE, LABELS))
        found = jnp.sum(to_slot_ref[:slots, :].astype(F32), axis=1, keepdims=True)
        reached[...] = jnp.broadcast_to(found, (slots, wide))

    drawn = jnp.dot(normed_ref[...], up_ref[...], preferred_element_type=F32) + bias_ref[...]
    size = jnp.maximum(drawn, 0.0) + jnp.log1p(jnp.exp(-jnp.abs(drawn)))
    act = act_ref[...].astype(F32)
    delta[...] = size
    driven[...] = size * act
    newest[...] = slots_ref[...].astype(F32)
    decay[...] = -jnp.exp(rate_ref[...])
    copies = wide // LABELS

    def one(slot, carry):
        base = decay[...]
        old = cache_ref[slot, :STATE, :].astype(F32)
        state = old
        for s in range(steps):
            at = s * slots + slot
            row = delta[pl.ds(at, 1), :]
            push = driven[pl.ds(at, 1), :]
            maps_in = jnp.concatenate([maps[at, :STATE, :]] * copies, axis=1)
            maps_out = jnp.concatenate([maps[at, STATE:, :]] * copies, axis=1)
            state = jnp.exp(row * base) * state + push * maps_in
            result[pl.ds(at, 1), :] = jnp.sum(maps_out * state, axis=0, keepdims=True)
        served = reached[pl.ds(slot, 1), :] > 0.5
        new_ref[slot, :STATE, :] = jnp.where(served, state, old).astype(BF16)
        kept = cache_ref[slot, STATE:, :].astype(F32)
        taken = jnp.concatenate(
            [newest[pl.ds(s * slots + slot, 1), :] for s in range(1, steps)], axis=0
        )
        new_ref[slot, STATE:, :] = jnp.where(served, taken, kept).astype(BF16)
        return carry

    lax.fori_loop(0, slots, one, 0)
    rows = gate_ref[...].astype(F32).reshape(total, wide).astype(BF16)
    gate = jnp.dot(to_slot_ref[...], rows, preferred_element_type=F32)
    gated = (result[...] + skip_ref[...] * act) * (gate / (1.0 + jnp.exp(-gate)))
    back = jnp.dot(to_arrival_ref[...], gated.astype(BF16), preferred_element_type=F32)
    out_ref[...] = back.reshape(out_ref.shape).astype(BF16)


def return_rows(owners, back_ref, result_ref, out_ref, landed, send_sem, recv_sem, local_sem):
    greet(owners, 1)
    for copy in spread(result_ref, landed, send_sem, recv_sem, local_sem, "pool", owners):
        copy.wait()
    total = back_ref.shape[1]
    for at in range(0, out_ref.shape[1], 512):
        rows = landed[:, :, at : at + 512].astype(F32).reshape(total, 512).astype(BF16)
        out_ref[:, at : at + 512] = jnp.dot(
            back_ref[...], rows, preferred_element_type=F32
        ).astype(BF16)


def local(
    projected_mixer,
    projected_gate,
    slot_state_cache,
    session_holder,
    session_slot,
    conversation_customer,
    filter_tap_weight,
    filter_bias,
    lowrank_step_weight,
    state_maps_weight,
    adapter_down_maps,
    adapter_up_maps,
    step_size_gain,
    step_up_weight,
    step_size_bias,
    log_decay_rates,
    skip_factor,
):
    owners, tp_count = lax.axis_size("pool"), lax.axis_size("tp")
    slots, depth, chans = slot_state_cache.shape
    served, steps, _ = projected_mixer.shape
    per_owner = slots // owners
    block = per_owner * steps
    total = slots * steps
    share = total // tp_count
    lanes = served * steps
    rank = lowrank_step_weight.shape[1]
    ranks = adapter_down_maps.shape[1]
    dma = pltpu.SemaphoreType.DMA
    shape = jax.ShapeDtypeStruct

    holder = jnp.repeat(session_holder, steps).reshape(1, lanes)
    slot = jnp.repeat(session_slot, steps).reshape(lanes, 1)
    tenant = jnp.repeat(conversation_customer, steps).reshape(lanes, 1)
    mixer = projected_mixer.reshape(lanes, chans)
    gate = projected_gate.reshape(lanes, chans)
    conv = jnp.swapaxes(slot_state_cache[:, STATE:, :], 0, 1)
    maps_weight = jnp.pad(state_maps_weight, ((0, 0), (0, LABELS - 2 * STATE)))

    arrived, back = pl.pallas_call(
        functools.partial(send_rows, owners, per_owner, steps),
        out_shape=(
            shape((owners, block, chans + LABELS), BF16),
            shape((lanes, total), BF16),
        ),
        in_specs=[whole_vmem()] * 4,
        out_specs=(whole_any(), whole_vmem()),
        scratch_shapes=[
            pltpu.VMEM((owners, block, chans + LABELS), BF16),
            dma((owners,)),
            dma((owners,)),
            dma,
        ],
        compiler_params=pltpu.CompilerParams(
            collective_id=0, has_side_effects=True, vmem_limit_bytes=VMEM_BYTES
        ),
        name="send_rows",
    )(holder, slot, tenant, mixer)

    wide = min(512, chans)
    part, by_slot, act, to_arrival, to_slot, mask = pl.pallas_call(
        functools.partial(project, steps, tp_count),
        grid=(chans // wide,),
        out_shape=(
            shape((tp_count, share, rank + LABELS), BF16),
            shape((total, chans), BF16),
            shape((total, chans), BF16),
            shape((total, total), BF16),
            shape((total, total), BF16),
            shape((total, LABELS), BF16),
        ),
        in_specs=[
            pl.BlockSpec((owners, block, wide), lambda c: (0, 0, c)),
            pl.BlockSpec((owners, block, LABELS), lambda c: (0, 0, chans // LABELS)),
            pl.BlockSpec((conv.shape[0], slots, wide), lambda c: (0, 0, c)),
            pl.BlockSpec((filter_tap_weight.shape[0], wide), lambda c: (0, c)),
            pl.BlockSpec((1, wide), lambda c: (0, c)),
            pl.BlockSpec((wide, rank), lambda c: (c, 0)),
            pl.BlockSpec((wide, LABELS), lambda c: (c, 0)),
            pl.BlockSpec((wide, ranks), lambda c: (c, 0)),
        ],
        out_specs=(
            fixed((tp_count, share, rank + LABELS)),
            pl.BlockSpec((total, wide), lambda c: (0, c)),
            pl.BlockSpec((total, wide), lambda c: (0, c)),
            fixed((total, total)),
            fixed((total, total)),
            fixed((total, LABELS)),
        ),
        scratch_shapes=[
            pltpu.VMEM((total, rank), F32),
            pltpu.VMEM((total, LABELS), F32),
            pltpu.VMEM((total, ranks), F32),
        ],
        compiler_params=pltpu.CompilerParams(vmem_limit_bytes=VMEM_BYTES),
        name="project",
    )(
        arrived,
        arrived,
        conv,
        filter_tap_weight,
        filter_bias.reshape(1, chans),
        lowrank_step_weight,
        maps_weight,
        adapter_down_maps,
    )

    arrived_gate, normed, tail = pl.pallas_call(
        functools.partial(join, owners, per_owner, steps, tp_count),
        out_shape=(
            shape((owners, block, chans), BF16),
            shape((tp_count, share, rank), BF16),
            shape((tp_count, share, LABELS), F32),
        ),
        in_specs=[whole_vmem()] * 6,
        out_specs=(whole_any(), whole_any(), whole_any()),
        scratch_shapes=[
            pltpu.VMEM((owners, block, chans), BF16),
            pltpu.VMEM((tp_count - 1, share, rank + LABELS), BF16),
            pltpu.VMEM((share, rank), BF16),
            pltpu.VMEM((share, LABELS), F32),
            dma((owners,)),
            dma((owners,)),
            dma,
            dma((tp_count,)),
            dma((tp_count,)),
            dma((tp_count,)),
            dma((tp_count,)),
            dma((tp_count,)),
            dma((tp_count,)),
            dma((2,)),
        ],
        compiler_params=pltpu.CompilerParams(
            collective_id=1, has_side_effects=True, vmem_limit_bytes=VMEM_BYTES
        ),
        name="join",
    )(
        holder,
        gate,
        part,
        mask.reshape(tp_count, share, LABELS),
        adapter_up_maps,
        step_size_gain.reshape(1, rank),
    )

    new_cache, result = pl.pallas_call(
        functools.partial(scan, steps),
        grid=(chans // wide,),
        out_shape=(
            shape((slots, depth, chans), BF16),
            shape((owners, block, chans), BF16),
        ),
        in_specs=[
            fixed((total, rank)),
            fixed((total, LABELS)),
            pl.BlockSpec((rank, wide), lambda c: (0, c)),
            pl.BlockSpec((1, wide), lambda c: (0, c)),
            pl.BlockSpec((STATE, wide), lambda c: (0, c)),
            pl.BlockSpec((1, wide), lambda c: (0, c)),
            pl.BlockSpec((total, wide), lambda c: (0, c)),
            pl.BlockSpec((total, wide), lambda c: (0, c)),
            pl.BlockSpec((owners, block, wide), lambda c: (0, 0, c)),
            fixed((total, total)),
            fixed((total, total)),
            pl.BlockSpec((slots, depth, wide), lambda c: (0, 0, c)),
        ],
        out_specs=(
            pl.BlockSpec((slots, depth, wide), lambda c: (0, 0, c)),
            pl.BlockSpec((owners, block, wide), lambda c: (0, 0, c)),
        ),
        scratch_shapes=[
            pltpu.VMEM((total, 2 * STATE, LABELS), F32),
            pltpu.VMEM((total, wide), F32),
            pltpu.VMEM((total, wide), F32),
            pltpu.VMEM((total, wide), F32),
            pltpu.VMEM((total, wide), F32),
            pltpu.VMEM((slots, wide), F32),
            pltpu.VMEM((STATE, wide), F32),
        ],
        compiler_params=pltpu.CompilerParams(vmem_limit_bytes=VMEM_BYTES),
        name="scan",
    )(
        normed.reshape(total, rank),
        tail.reshape(total, LABELS),
        step_up_weight,
        step_size_bias.reshape(1, chans),
        log_decay_rates,
        skip_factor.reshape(1, chans),
        act,
        by_slot,
        arrived_gate,
        to_arrival,
        to_slot,
        slot_state_cache,
    )

    gated = pl.pallas_call(
        functools.partial(return_rows, owners),
        out_shape=shape((lanes, chans), BF16),
        in_specs=[whole_vmem()] * 2,
        out_specs=whole_vmem(),
        scratch_shapes=[
            pltpu.VMEM((owners, block, chans), BF16),
            dma((owners,)),
            dma((owners,)),
            dma,
        ],
        compiler_params=pltpu.CompilerParams(
            collective_id=2, has_side_effects=True, vmem_limit_bytes=VMEM_BYTES
        ),
        name="return_rows",
    )(back, result)
    return (gated.reshape(served, steps, chans), new_cache)


def solution(mesh):
    placed = (
        P("pool", None, "tp"),
        P("pool", None, "tp"),
        P("pool", None, "tp"),
        P("pool"),
        P("pool"),
        P("pool"),
        P(None, "tp"),
        P("tp"),
        P("tp", None),
        P("tp", None),
        P("tp", None),
        P(),
        P(),
        P(None, "tp"),
        P("tp"),
        P(None, "tp"),
        P("tp"),
    )
    return jax.shard_map(
        local,
        mesh=mesh,
        in_specs=placed,
        out_specs=(P("pool", None, "tp"), P("pool", None, "tp")),
        check_vma=False,
    )
```

time: 300 us -> 111 us (0.37)
  waiting for transfers between devices: 128 us -> 0 us
  Pallas kernels: 0 us -> 85.4 us
  matrix products: 36.5 us -> 0 us
  other arithmetic: 31.3 us -> 0.01 us
  local copies, waits for them, and re-layouts: 53.9 us -> 23.9 us
  blocking collectives: 19.2 us -> 0 us
  starting transfers between devices: 14.8 us -> 0 us
  between operations: 14.5 us -> 0.81 us
    all_to_all x3 -> x0, waiting for transfers between devices: 100 us -> none  [the longest x1 50.6 us: local(): lax.all_to_all(outgoing.reshape(owners, per_owner, depth_rows, chan_count...]
    pallas_call x0 -> x5, Pallas kernels: none -> 85.4 us  [the longest x1 24.7 us: local(): pl.pallas_call(functools.partial(scan, steps), grid=(chans // wide,), out...]
    dot_general x9 -> x0, matrix products: 36.5 us -> none  [the longest x2 11 us: take_rows(): jnp.dot(selector, flattened, preferred_element_type=jnp.float32)]
    psum x1 -> x0, waiting for transfers between devices: 27.9 us -> none  [mixer_rows(): lax.psum((part_low, part_maps, part_adapt), 'tp')]
    reshape x6 -> x3, local copies, waits for them, and re-layouts: 24.2 us -> 3.33 us  [the longest x1 1.17 us: local(): mixer = projected_mixer.reshape(lanes, chans)]
    psum x1 -> x0, blocking collectives: 19.2 us -> none  [mixer_rows(): lax.psum((part_low, part_maps, part_adapt), 'tp')]
    all_to_all x3 -> x0, starting transfers between devices: 14.8 us -> none  [the longest x1 5.17 us: local(): lax.all_to_all(request_slot.reshape(owners, per_owner), 'pool', split_axi...]
    select_n x1 -> x0, other arithmetic: 12.6 us -> none  [write_rows(): return jnp.where(reached[:, None, None], placed, table)]
  transfers between devices with their start and end apart: 4 -> 0, of which waited for: 3 -> 0; matrix products, arithmetic and copies ran while one was open for 8% -> 0% of each run, Pallas kernels for 0% -> 0%
where the time goes in v2:
time: 111 us; the launch traced here: 110 us
  Pallas kernels  85.4 us (77%)
  local copies, waits for them, and re-layouts  23.9 us (22%)
    pallas_call x1, Pallas kernels, local(): pl.pallas_call(functools.partial(scan, steps), grid=(chans // wide,), out...  24.7 us
    pallas_call x1, Pallas kernels, local(): pl.pallas_call(functools.partial(join, owners, per_owner, steps, tp_count...  22.6 us
    pallas_call x1, Pallas kernels, local(): pl.pallas_call(functools.partial(send_rows, owners, per_owner, steps), ou...  17.1 us
    unnamed x25, local copies, waits for them, and re-layouts  16.6 us
    pallas_call x1, Pallas kernels, local(): pl.pallas_call(functools.partial(return_rows, owners), out_shape=shape((l...  13.8 us
    pallas_call x1, Pallas kernels, local(): pl.pallas_call(functools.partial(project, steps, tp_count), grid=(chans /...  7.21 us

profile of v2, /device:TPU:0, one launch (start us, length us, event | category | flops | bytes accessed | tf_op | source)
XLA Modules:
  0.0 110.1 jit_solution(9594077832930770662)
XLA Ops:
  0.7 0.7 broadcast_in_dim.9
  1.4 0.1 reshape_reshape.9.holder_ref
  1.5 0.7 broadcast_in_dim.10
  2.2 0.7 broadcast_in_dim.11
  2.9 0.1 reshape_reshape.13.tenant_ref
  3.0 0.1 reshape_reshape.12.slot_ref
  3.1 1.2 %reshape.34.rows_ref = bf16[128,2048]{1,0:T(8,128)(2,1)S(1)} reshape(bf16[32,4,2048]{2,1,0:T(4,128)(2,1)} %param.17) | data formatting | bytes 1048576 | tf_op jit(solution)/shard_map/reshape | solution.py:441
  4.3 1.2 %reshape.35.gate_ref = bf16[128,2048]{1,0:T(8,128)(2,1)S(1)} reshape(bf16[32,4,2048]{2,1,0:T(4,128)(2,1)} %param.18) | data formatting | bytes 1048576 | tf_op jit(solution)/shard_map/reshape | solution.py:442
  5.4 1.2 %copy.26 = bf16[2048,32]{1,0:T(8,128)(2,1)S(1)} copy(bf16[2048,32]{0,1:T(8,128)(2,1)} %param.26) | data formatting | bytes 262144 | tf_op args[9]
  6.6 0.1 pad.4.maps_ref
  6.7 17.1 %send_rows.1 = (bf16[8,32,2176]{2,1,0:T(8,128)(2,1)S(1)}, bf16[128,256]{1,0:T(8,128)(2,1)S(1)}) custom-call(s32[1,128]{1,0:T(1,128)S(1)} %reshape_reshape.9.holder_ref, s32[128,1]{1,0:T(8,128)S(1)} %reshape_reshape.12.slot_ref, s32[128,1]{1,0:T(8,128)S(1)} %reshape_reshape.13.tenant_ref, bf16[128,2048]{1,0:T(8,128)(2,1)S(1)} %reshape.34.rows_ref), custom_call_target="tpu_custom_call" | custom-call | tf_op jit(solution)/shard_map/send_rows/pallas_call | solution.py:446
  23.9 0.0 copy-start
  23.9 1.0 copy-done
  24.9 1.3 %slice_bitcast_fusion.conv_ref = bf16[3,64,2048]{2,1,0:T(8,128)(2,1)S(1)} fusion(bf16[64,19,2048]{2,0,1:T(8,128)(2,1)} %param.19), kind=kLoop, calls=%fused_computation | loop fusion | bytes 1572864 | tf_op jit(solution)/shard_map/transpose | solution.py:443
  26.3 0.0 slice-start.1
  26.3 7.2 %project.1 = (bf16[4,64,640]{2,1,0:T(8,128)(2,1)S(1)}, bf16[256,2048]{1,0:T(8,128)(2,1)S(1)}, bf16[256,2048]{1,0:T(8,128)(2,1)S(1)}, bf16[256,256]{1,0:T(8,128)(...) custom-call(bf16[8,32,2176]{2,1,0:T(8,128)(2,1)} %copy-done, bf16[8,32,2176]{2,1,0:T(8,128)(2,1)} %copy-done, ...), custom_call_target="tpu_custom_call" | custom-call | tf_op jit(solution)/shard_map/project/pallas_call | solution.py:467
  33.5 22.6 %join.1 = (bf16[8,32,2048]{2,1,0:T(8,128)(2,1)S(1)}, bf16[4,64,512]{2,1,0:T(8,128)(2,1)S(1)}, f32[4,64,128]{2,1,0:T(8,128)S(1)}) custom-call(s32[1,128]{1,0:T(1,128)S(1)} %reshape_reshape.9.holder_ref, bf16[128,2048]{1,0:T(8,128)(2,1)S(1)} %reshape.35.gate_ref, bf16[4,64,640]{2,1,0:T(8,128)(2,1)S(1)} %get-tuple-element.17.part_ref, ...), custom_call_target="tpu_custom_call" | custom-call | tf_op jit(solution)/shard_map/join/pallas_call | solution.py:514
  56.1 1.0 copy-done.1
  57.1 0.0 copy-start.5
  57.1 5.5 %copy.27.cache_ref = bf16[64,19,2048]{2,1,0:T(8,128)(2,1)} copy(bf16[64,19,2048]{2,0,1:T(8,128)(2,1)S(1)} %bitcast.17) | data formatting | bytes 9961472 | tf_op args[2]
  62.7 24.7 %scan.1 = (bf16[64,19,2048]{2,1,0:T(8,128)(2,1)}, bf16[8,32,2048]{2,1,0:T(8,128)(2,1)S(1)}) custom-call(bf16[256,512]{1,0:T(8,128)(2,1)S(1)} %bitcast.9, f32[256,128]{1,0:T(8,128)S(1)} %bitcast.10, bf16[512,2048]{1,0:T(8,128)(2,1)} %up_ref.3, f32[1,2048]{1,0:T(1,128)S(1)} %bitcast.12, f32[16,2048]{1,0:T(8,128)S(1)} %copy-done.3, f32[1,2048]{1,0:T(1,128)S(1)} %bitcast.13, ...), custom_call_target="tpu_custom_call" | custom-call | tf_op jit(solution)/shard_map/scan/pallas_call | solution.py:552
  87.4 13.8 %return_rows.1 = bf16[128,2048]{1,0:T(8,128)(2,1)S(1)} custom-call(bf16[128,256]{1,0:T(8,128)(2,1)S(1)} %get-tuple-element.15.back_ref, bf16[8,32,2048]{2,1,0:T(8,128)(2,1)S(1)} %get-tuple-element.26.result_ref), custom_call_target="tpu_custom_call" | custom-call | tf_op jit(solution)/shard_map/return_rows/pallas_call | solution.py:603
  101.2 1.0 reshape.43
  102.2 7.9 %copy.28 = bf16[64,19,2048]{2,0,1:T(8,128)(2,1)} copy(bf16[64,19,2048]{2,1,0:T(8,128)(2,1)} %get-tuple-element.31) | data formatting | bytes 9961472
  (18 shorter events, 0.0 us)
Async XLA Ops:
  0.6 25.6 %copy-start.7 = (f32[2048]{0:T(1024)S(1)}, f32[2048]{0:T(1024)}, u32[]{:S(2)}) copy-start(f32[2048]{0:T(1024)} %param.24) | copy-start | bytes 24580
  0.6 25.6 %copy-start.4 = (f32[4,2048]{1,0:T(4,128)S(1)}, f32[4,2048]{1,0:T(4,128)}, u32[]{:S(2)}) copy-start(f32[4,2048]{1,0:T(4,128)} %tap_ref.1) | copy-start | bytes 98308
  23.9 1.0 copy-start
  24.9 32.2 %slice-start = ((s8[4980736]{0:T(1024)(128)(4,1)}), s8[4194304]{0:T(1024)(128)(4,1)S(1)}, s32[]{:S(2)}) async-start(s8[4980736]{0:T(1024)(128)(4,1)} %bitcast.16), calls=%async_computation | async-start | bytes 8388608
  26.2 7.3 %copy-start.2 = (bf16[1024,512]{1,0:T(8,128)(2,1)S(1)}, bf16[1024,512]{1,0:T(8,128)(2,1)}, u32[]{:S(2)}) copy-start(bf16[1024,512]{1,0:T(8,128)(2,1)} %up_ref.2) | copy-start | bytes 3145732
  26.3 7.3 %copy-start.8 = (f32[512]{0:T(512)S(1)}, f32[512]{0:T(512)}, u32[]{:S(2)}) copy-start(f32[512]{0:T(512)} %param.29) | copy-start | bytes 6148
  26.3 30.8 %slice-start.1 = ((s8[4980736]{0:T(1024)(128)(4,1)}), s8[786432]{0:T(1024)(128)(4,1)S(1)}, s32[]{:S(2)}) async-start(s8[4980736]{0:T(1024)(128)(4,1)} %bitcast.16), calls=%async_computation.1 | async-start | bytes 1572864
  56.1 1.0 copy-start.1
  57.1 5.6 %copy-start.3 = (f32[16,2048]{1,0:T(8,128)S(1)}, f32[16,2048]{1,0:T(8,128)}, u32[]{:S(2)}) copy-start(f32[16,2048]{1,0:T(8,128)} %rate_ref.1) | copy-start | bytes 393220
  57.1 5.6 %copy-start.5 = (f32[2048]{0:T(1024)S(1)}, f32[2048]{0:T(1024)}, u32[]{:S(2)}) copy-start(f32[2048]{0:T(1024)} %param.31) | copy-start | bytes 24580
  57.1 5.6 %copy-start.6 = (f32[2048]{0:T(1024)S(1)}, f32[2048]{0:T(1024)}, u32[]{:S(2)}) copy-start(f32[2048]{0:T(1024)} %param.33) | copy-start | bytes 24580

commit v3 on v2

--- a/solution.py
+++ b/solution.py
@@ -12,6 +12,7 @@
 TENANT_COUNT = 64
 LABELS = 128
 VMEM_BYTES = 50 * 1024 * 1024
+LOG2_E = 1.4426950408889634
 F32 = jnp.float32
 BF16 = jnp.bfloat16
 
@@ -36,16 +37,24 @@
     return pl.BlockSpec(shape, lambda c: (0,) * len(shape))
 
 
+def per_lane(numbers, steps):
+    rows = numbers.shape[1]
+    shape = (rows, rows * steps)
+    wide = as_bf16(iota(shape, 0) == iota(shape, 1) // steps)
+    return jnp.dot(numbers.astype(F32).astype(BF16), wide, preferred_element_type=F32)
+
+
 def dispatch_matrix(holder, owners, per_owner, steps):
-    lanes = holder.shape[1]
-    named = jnp.where(iota((owners, lanes), 0) == holder, 1.0, 0.0)
+    lanes = holder.shape[1] * steps
+    holder = per_lane(holder, steps)
+    named = jnp.where(iota((owners, lanes), 0).astype(F32) == holder, 1.0, 0.0)
     earlier = as_bf16(
         (iota((lanes, lanes), 0) // steps < iota((lanes, lanes), 1) // steps)
         & (iota((lanes, lanes), 0) % steps == 0)
     )
     before = jnp.dot(named.astype(BF16), earlier, preferred_element_type=F32)
     rank = jnp.sum(named * before, axis=0, keepdims=True)
-    target = holder.astype(F32) * per_owner + rank
+    target = holder * per_owner + rank
     shape = (owners * per_owner * steps, lanes)
     return jnp.where(
         ((iota(shape, 0) // steps).astype(F32) == target)
@@ -56,6 +65,17 @@
 
 
 def greet(pool_count, tp_count):
+    announce(pool_count, tp_count)
+    await_all(pool_count, tp_count)
+
+
+def await_all(pool_count, tp_count):
+    pl.semaphore_wait(
+        pltpu.get_barrier_semaphore(), max(pool_count - 1, 0) + max(tp_count - 1, 0)
+    )
+
+
+def announce(pool_count, tp_count):
     barrier = pltpu.get_barrier_semaphore()
     me, mine = lax.axis_index("pool"), lax.axis_index("tp")
     for k in range(1, pool_count):
@@ -72,7 +92,6 @@
             device_id={"tp": lax.rem(mine + k, tp_count)},
             device_id_type=pl.DeviceIdType.MESH,
         )
-    pl.semaphore_wait(barrier, max(pool_count - 1, 0) + max(tp_count - 1, 0))
 
 
 def spread(source, landing, send_sem, recv_sem, local_sem, axis, count):
@@ -119,18 +138,24 @@
     recv_sem,
     local_sem,
 ):
+    announce(owners, 1)
     picked = dispatch_matrix(holder_ref[...], owners, per_owner, steps)
     selector = picked.astype(BF16)
     back_ref[...] = picked.T.astype(BF16)
     lanes = rows_ref.shape[0]
     chans = rows_ref.shape[1]
     slots = owners * per_owner
-    column = iota((lanes, LABELS), 1)
-    labels = as_bf16((column == slot_ref[...]) | (column == tenant_ref[...] + slots))
-    marked = jnp.dot(selector, labels, preferred_element_type=F32)
+    line = iota((LABELS, lanes), 0).astype(F32)
+    labels = as_bf16(
+        (line == per_lane(slot_ref[...], steps))
+        | (line == per_lane(tenant_ref[...], steps) + slots)
+    )
+    marked = lax.dot_general(
+        selector, labels, (((1,), (1,)), ((), ())), preferred_element_type=F32
+    )
     outgoing[:, :, chans:] = marked.reshape(owners, per_owner * steps, LABELS).astype(BF16)
     pick_rows(selector, rows_ref, outgoing)
-    greet(owners, 1)
+    await_all(owners, 1)
     for copy in spread(outgoing, arrived_ref, send_sem, recv_sem, local_sem, "pool", owners):
         copy.wait()
 
@@ -139,8 +164,9 @@
     steps,
     tp_count,
     arrived_ref,
-    label_ref,
-    conv_ref,
+    conv_ref0,
+    conv_ref1,
+    conv_ref2,
     tap_ref,
     bias_ref,
     low_ref,
@@ -157,13 +183,13 @@
     down_acc,
 ):
     chunk = pl.program_id(0)
-    slots = conv_ref.shape[1]
+    slots, wide = conv_ref0.shape[1:]
     total = slots * steps
-    wide = act_ref.shape[1]
+    chans = arrived_ref.shape[2] - LABELS
 
     @pl.when(chunk == 0)
     def _():
-        labels = label_ref[...].astype(F32).reshape(total, LABELS)
+        labels = arrived_ref[:, :, chans:].astype(F32).reshape(total, LABELS)
         lane = iota((LABELS, total), 0)
         expand = as_bf16(lane == iota((LABELS, total), 1) % slots)
         selected = jnp.dot(labels.astype(BF16), expand, preferred_element_type=F32)
@@ -180,10 +206,11 @@
         maps_acc[...] = jnp.zeros_like(maps_acc)
         down_acc[...] = jnp.zeros_like(down_acc)
 
-    rows = arrived_ref[...].astype(F32).reshape(total, wide).astype(BF16)
+    columns = pl.ds(pl.multiple_of(chunk * wide, wide), wide)
+    rows = arrived_ref[:, :, columns].astype(F32).reshape(total, wide).astype(BF16)
     mixed = jnp.dot(to_slot_ref[...], rows, preferred_element_type=F32)
     slots_ref[...] = mixed.astype(BF16)
-    window = [conv_ref[k].astype(F32) for k in range(conv_ref.shape[0])]
+    window = [conv_ref[0].astype(F32) for conv_ref in (conv_ref0, conv_ref1, conv_ref2)]
     window += [mixed[s * slots : (s + 1) * slots] for s in range(steps)]
     for s in range(steps):
         summed = jnp.broadcast_to(bias_ref[...], (slots, wide))
@@ -192,7 +219,9 @@
         act_ref[s * slots : (s + 1) * slots, :] = (summed / (1.0 + jnp.exp(-summed))).astype(BF16)
     act = act_ref[...]
     low_acc[...] += jnp.dot(act, low_ref[...], preferred_element_type=F32)
-    maps_acc[...] += jnp.dot(act, maps_ref[...], preferred_element_type=F32)
+    maps_acc[:, : 2 * STATE] += lax.dot_general(
+        act, maps_ref[...], (((1,), (1,)), ((), ())), preferred_element_type=F32
+    )
     down_acc[...] += jnp.dot(act, down_ref[...], preferred_element_type=F32)
 
     @pl.when(chunk == pl.num_programs(0) - 1)
@@ -336,55 +365,59 @@
     maps,
     delta,
     driven,
-    newest,
     result,
     reached,
     decay,
 ):
-    slots = cache_ref.shape[0]
+    slots, wide = cache_ref.shape[1:]
     total = slots * steps
-    wide = act_ref.shape[1]
-
-    @pl.when(pl.program_id(0) == 0)
+    group, tile = 16, LABELS
+    tiles = wide // tile
+    chunk = pl.program_id(0)
+
+    @pl.when(chunk == 0)
     def _():
-        turned = tail_ref[...].T
-        for at in range(total):
-            maps[at] = jnp.broadcast_to(turned[: 2 * STATE, at : at + 1], (2 * STATE, LABELS))
+        for n in range(2 * STATE):
+            maps[n] = jnp.broadcast_to(tail_ref[:, n : n + 1], (total, LABELS))
         found = jnp.sum(to_slot_ref[:slots, :].astype(F32), axis=1, keepdims=True)
-        reached[...] = jnp.broadcast_to(found, (slots, wide))
+        reached[...] = jnp.broadcast_to(found, (slots, LABELS))
 
     drawn = jnp.dot(normed_ref[...], up_ref[...], preferred_element_type=F32) + bias_ref[...]
     size = jnp.maximum(drawn, 0.0) + jnp.log1p(jnp.exp(-jnp.abs(drawn)))
     act = act_ref[...].astype(F32)
     delta[...] = size
     driven[...] = size * act
-    newest[...] = slots_ref[...].astype(F32)
-    decay[...] = -jnp.exp(rate_ref[...])
-    copies = wide // LABELS
-
-    def one(slot, carry):
-        base = decay[...]
-        old = cache_ref[slot, :STATE, :].astype(F32)
-        state = old
+    decay[...] = jnp.exp(rate_ref[...]) * -LOG2_E
+
+    def one(place, carry):
+        first = place // tiles * group
+        rows = pl.ds(pl.multiple_of(first, group), group)
+        cols = pl.ds(pl.multiple_of(lax.rem(place, tiles) * tile, tile), tile)
+        at = [pl.ds(pl.multiple_of(s * slots + first, group), group) for s in range(steps)]
+        sizes = [delta[at[s], cols] for s in range(steps)]
+        pushes = [driven[at[s], cols] for s in range(steps)]
+        served = reached[rows, :] > 0.5
+        sums = [jnp.zeros((group, tile), F32)] * steps
+        for n in range(STATE):
+            old = cache_ref[n, rows, cols].astype(F32)
+            base = decay[n : n + 1, cols]
+            state = old
+            for s in range(steps):
+                state = jnp.exp2(sizes[s] * base) * state + pushes[s] * maps[n, at[s], :]
+                sums[s] = sums[s] + maps[STATE + n, at[s], :] * state
+            new_ref[n, rows, cols] = jnp.where(served, state, old).astype(BF16)
         for s in range(steps):
-            at = s * slots + slot
-            row = delta[pl.ds(at, 1), :]
-            push = driven[pl.ds(at, 1), :]
-            maps_in = jnp.concatenate([maps[at, :STATE, :]] * copies, axis=1)
-            maps_out = jnp.concatenate([maps[at, STATE:, :]] * copies, axis=1)
-            state = jnp.exp(row * base) * state + push * maps_in
-            result[pl.ds(at, 1), :] = jnp.sum(maps_out * state, axis=0, keepdims=True)
-        served = reached[pl.ds(slot, 1), :] > 0.5
-        new_ref[slot, :STATE, :] = jnp.where(served, state, old).astype(BF16)
-        kept = cache_ref[slot, STATE:, :].astype(F32)
-        taken = jnp.concatenate(
-            [newest[pl.ds(s * slots + slot, 1), :] for s in range(1, steps)], axis=0
-        )
-        new_ref[slot, STATE:, :] = jnp.where(served, taken, kept).astype(BF16)
+            result[at[s], cols] = sums[s]
+        kept = cache_ref.shape[0] - STATE
+        for k in range(kept):
+            taken = slots_ref[at[steps - kept + k], cols].astype(F32)
+            old = cache_ref[STATE + k, rows, cols].astype(F32)
+            new_ref[STATE + k, rows, cols] = jnp.where(served, taken, old).astype(BF16)
         return carry
 
-    lax.fori_loop(0, slots, one, 0)
-    rows = gate_ref[...].astype(F32).reshape(total, wide).astype(BF16)
+    lax.fori_loop(0, slots // group * tiles, one, 0)
+    columns = pl.ds(pl.multiple_of(chunk * wide, wide), wide)
+    rows = gate_ref[:, :, columns].astype(F32).reshape(total, wide).astype(BF16)
     gate = jnp.dot(to_slot_ref[...], rows, preferred_element_type=F32)
     gated = (result[...] + skip_ref[...] * act) * (gate / (1.0 + jnp.exp(-gate)))
     back = jnp.dot(to_arrival_ref[...], gated.astype(BF16), preferred_element_type=F32)
@@ -435,13 +468,16 @@
     dma = pltpu.SemaphoreType.DMA
     shape = jax.ShapeDtypeStruct
 
-    holder = jnp.repeat(session_holder, steps).reshape(1, lanes)
-    slot = jnp.repeat(session_slot, steps).reshape(lanes, 1)
-    tenant = jnp.repeat(conversation_customer, steps).reshape(lanes, 1)
+    holder = session_holder.reshape(1, served)
+    slot = session_slot.reshape(1, served)
+    tenant = conversation_customer.reshape(1, served)
     mixer = projected_mixer.reshape(lanes, chans)
     gate = projected_gate.reshape(lanes, chans)
-    conv = jnp.swapaxes(slot_state_cache[:, STATE:, :], 0, 1)
-    maps_weight = jnp.pad(state_maps_weight, ((0, 0), (0, LABELS - 2 * STATE)))
+    cache = jnp.swapaxes(slot_state_cache, 0, 1)
+    maps_weight = state_maps_weight.T
+
+    def conv_row(k):
+        return pl.BlockSpec((1, slots, wide), lambda c: (k, 0, c))
 
     arrived, back = pl.pallas_call(
         functools.partial(send_rows, owners, per_owner, steps),
@@ -476,13 +512,14 @@
             shape((total, LABELS), BF16),
         ),
         in_specs=[
-            pl.BlockSpec((owners, block, wide), lambda c: (0, 0, c)),
-            pl.BlockSpec((owners, block, LABELS), lambda c: (0, 0, chans // LABELS)),
-            pl.BlockSpec((conv.shape[0], slots, wide), lambda c: (0, 0, c)),
+            whole_vmem(),
+            conv_row(depth - 3),
+            conv_row(depth - 2),
+            conv_row(depth - 1),
             pl.BlockSpec((filter_tap_weight.shape[0], wide), lambda c: (0, c)),
             pl.BlockSpec((1, wide), lambda c: (0, c)),
             pl.BlockSpec((wide, rank), lambda c: (c, 0)),
-            pl.BlockSpec((wide, LABELS), lambda c: (c, 0)),
+            pl.BlockSpec((2 * STATE, wide), lambda c: (0, c)),
             pl.BlockSpec((wide, ranks), lambda c: (c, 0)),
         ],
         out_specs=(
@@ -502,8 +539,9 @@
         name="project",
     )(
         arrived,
-        arrived,
-        conv,
+        cache,
+        cache,
+        cache,
         filter_tap_weight,
         filter_bias.reshape(1, chans),
         lowrank_step_weight,
@@ -553,7 +591,7 @@
         functools.partial(scan, steps),
         grid=(chans // wide,),
         out_shape=(
-            shape((slots, depth, chans), BF16),
+            shape((depth, slots, chans), BF16),
             shape((owners, block, chans), BF16),
         ),
         in_specs=[
@@ -565,22 +603,21 @@
             pl.BlockSpec((1, wide), lambda c: (0, c)),
             pl.BlockSpec((total, wide), lambda c: (0, c)),
             pl.BlockSpec((total, wide), lambda c: (0, c)),
-            pl.BlockSpec((owners, block, wide), lambda c: (0, 0, c)),
+            whole_vmem(),
             fixed((total, total)),
             fixed((total, total)),
-            pl.BlockSpec((slots, depth, wide), lambda c: (0, 0, c)),
+            pl.BlockSpec((depth, slots, wide), lambda c: (0, 0, c)),
         ],
         out_specs=(
-            pl.BlockSpec((slots, depth, wide), lambda c: (0, 0, c)),
+            pl.BlockSpec((depth, slots, wide), lambda c: (0, 0, c)),
             pl.BlockSpec((owners, block, wide), lambda c: (0, 0, c)),
         ),
         scratch_shapes=[
-            pltpu.VMEM((total, 2 * STATE, LABELS), F32),
+            pltpu.VMEM((2 * STATE, total, LABELS), F32),
             pltpu.VMEM((total, wide), F32),
             pltpu.VMEM((total, wide), F32),
             pltpu.VMEM((total, wide), F32),
-            pltpu.VMEM((total, wide), F32),
-            pltpu.VMEM((slots, wide), F32),
+            pltpu.VMEM((slots, LABELS), F32),
             pltpu.VMEM((STATE, wide), F32),
         ],
         compiler_params=pltpu.CompilerParams(vmem_limit_bytes=VMEM_BYTES),
@@ -597,7 +634,7 @@
         arrived_gate,
         to_arrival,
         to_slot,
-        slot_state_cache,
+        cache,
     )
 
     gated = pl.pallas_call(
@@ -616,7 +653,7 @@
         ),
         name="return_rows",
     )(back, result)
-    return (gated.reshape(served, steps, chans), new_cache)
+    return (gated.reshape(served, steps, chans), jnp.swapaxes(new_cache, 0, 1))
 
 
 def solution(mesh):

time: 111 us -> 89.3 us (0.80)
  local copies, waits for them, and re-layouts: 23.9 us -> 8.62 us
  Pallas kernels: 85.4 us -> 78.9 us
    unnamed x25 -> x24, local copies, waits for them, and re-layouts: 16.6 us -> 5.31 us
    pallas_call x1, Pallas kernels: 24.7 us -> 18.8 us  [local(): pl.pallas_call(functools.partial(scan, steps), grid=(chans // wide,), out...]
    broadcast_in_dim x3 -> x0, local copies, waits for them, and re-layouts: 2.19 us -> none  [the longest x1 0.74 us: local(): holder = jnp.repeat(session_holder, steps).reshape(1, lanes)]
    transpose x1 -> x0, local copies, waits for them, and re-layouts: 1.35 us -> none  [local(): conv = jnp.swapaxes(slot_state_cache[:, STATE:, :], 0, 1)]
where the time goes in v3:
time: 89.3 us; the launch traced here: 88.3 us
  Pallas kernels  78.9 us (88%)
  local copies, waits for them, and re-layouts  8.62 us (10%)
    pallas_call x1, Pallas kernels, local(): pl.pallas_call(functools.partial(join, owners, per_owner, steps, tp_count...  22.5 us
    pallas_call x1, Pallas kernels, local(): pl.pallas_call(functools.partial(scan, steps), grid=(chans // wide,), out...  18.8 us
    pallas_call x1, Pallas kernels, local(): pl.pallas_call(functools.partial(send_rows, owners, per_owner, steps), ou...  16.6 us
    pallas_call x1, Pallas kernels, local(): pl.pallas_call(functools.partial(return_rows, owners), out_shape=shape((l...  13.9 us
    pallas_call x1, Pallas kernels, local(): pl.pallas_call(functools.partial(project, steps, tp_count), grid=(chans /...  7.12 us
    unnamed x24, local copies, waits for them, and re-layouts  5.31 us

profile of v3, /device:TPU:0, one launch (start us, length us, event | category | flops | bytes accessed | tf_op | source)
XLA Modules:
  0.0 88.3 jit_solution(14380816032132377687)
XLA Ops:
  0.6 1.2 %reshape.46.rows_ref = bf16[128,2048]{1,0:T(8,128)(2,1)S(1)} reshape(bf16[32,4,2048]{2,1,0:T(4,128)(2,1)} %param.17) | data formatting | bytes 1048576 | tf_op jit(solution)/shard_map/reshape | solution.py:474
  1.8 1.2 %reshape.47.gate_ref = bf16[128,2048]{1,0:T(8,128)(2,1)S(1)} reshape(bf16[32,4,2048]{2,1,0:T(4,128)(2,1)} %param.18) | data formatting | bytes 1048576 | tf_op jit(solution)/shard_map/reshape | solution.py:475
  3.0 0.0 copy-start.9
  3.0 0.6 copy-done.9
  3.6 0.7 copy-done.10
  4.3 0.7 copy-done.11
  4.9 16.6 %send_rows.1 = (bf16[8,32,2176]{2,1,0:T(8,128)(2,1)S(1)}, bf16[128,256]{1,0:T(8,128)(2,1)S(1)}) custom-call(s32[1,32]{1,0:T(1,128)S(1)} %bitcast.21, s32[1,32]{1,0:T(1,128)S(1)} %bitcast.23, s32[1,32]{1,0:T(1,128)S(1)} %bitcast.24, bf16[128,2048]{1,0:T(8,128)(2,1)S(1)} %reshape.46.rows_ref), custom_call_target="tpu_custom_call" | custom-call | tf_op jit(solution)/shard_map/send_rows/pallas_call | solution.py:482
  21.5 0.0 copy-start.2
  21.5 0.9 %copy-done.2 = bf16[2048,32]{0,1:T(8,128)(2,1)S(1)} copy-done((bf16[2048,32]{0,1:T(8,128)(2,1)S(1)}, bf16[2048,32]{0,1:T(8,128)(2,1)}, u32[]{:S(2)}) %copy-start.2) | copy-done | bytes 131096
  22.4 0.8 copy-done.4
  23.2 0.7 copy-done.5
  23.9 0.0 copy-start.7
  23.9 7.1 %project.1 = (bf16[4,64,640]{2,1,0:T(8,128)(2,1)S(1)}, bf16[256,2048]{1,0:T(8,128)(2,1)S(1)}, bf16[256,2048]{1,0:T(8,128)(2,1)S(1)}, bf16[256,256]{1,0:T(8,128)(...) custom-call(bf16[8,32,2176]{2,1,0:T(8,128)(2,1)S(1)} %get-tuple-element.16.arrived_ref, ...), custom_call_target="tpu_custom_call" | custom-call | tf_op jit(solution)/shard_map/project/pallas_call | solution.py:503
  31.0 0.0 copy-done
  31.0 0.0 copy-done.8
  31.0 22.5 %join.1 = (bf16[8,32,2048]{2,1,0:T(8,128)(2,1)S(1)}, bf16[4,64,512]{2,1,0:T(8,128)(2,1)S(1)}, f32[4,64,128]{2,1,0:T(8,128)S(1)}) custom-call(s32[1,32]{1,0:T(1,128)S(1)} %bitcast.22, bf16[128,2048]{1,0:T(8,128)(2,1)S(1)} %reshape.47.gate_ref, bf16[4,64,640]{2,1,0:T(8,128)(2,1)S(1)} %get-tuple-element.17.part_ref, bf16[4,64,128]{2,1,0:T(8,128)(2,1)S(1)} %bitcast.16, ...), custom_call_target="tpu_custom_call" | custom-call | tf_op jit(solution)/shard_map/join/pallas_call | solution.py:552
  53.6 0.0 copy-start.1
  53.6 1.0 %copy-done.1 = bf16[8,32,2048]{2,1,0:T(8,128)(2,1)} copy-done((bf16[8,32,2048]{2,1,0:T(8,128)(2,1)}, bf16[8,32,2048]{2,1,0:T(8,128)(2,1)S(1)}, u32[]{:S(2)}) %copy-start.1) | copy-done | bytes 1048600
  54.5 0.0 copy-done.3
  54.6 0.0 copy-done.6
  54.6 0.0 copy-done.7
  54.6 18.8 %scan.1 = (bf16[19,64,2048]{2,1,0:T(8,128)(2,1)}, bf16[8,32,2048]{2,1,0:T(8,128)(2,1)S(1)}) custom-call(bf16[256,512]{1,0:T(8,128)(2,1)S(1)} %bitcast.13, f32[256,128]{1,0:T(8,128)S(1)} %bitcast.15, bf16[512,2048]{1,0:T(8,128)(2,1)} %up_ref.3, f32[1,2048]{1,0:T(1,128)S(1)} %bitcast.18, f32[16,2048]{1,0:T(8,128)S(1)} %copy-done.3, f32[1,2048]{1,0:T(1,128)S(1)} %bitcast.19, ...), custom_call_target="tpu_custom_call" | custom-call | tf_op jit(solution)/shard_map/scan/pallas_call | solution.py:590
  73.4 13.9 %return_rows.1 = bf16[128,2048]{1,0:T(8,128)(2,1)S(1)} custom-call(bf16[128,256]{1,0:T(8,128)(2,1)S(1)} %get-tuple-element.15.back_ref, bf16[8,32,2048]{2,1,0:T(8,128)(2,1)S(1)} %get-tuple-element.26.result_ref), custom_call_target="tpu_custom_call" | custom-call | tf_op jit(solution)/shard_map/return_rows/pallas_call | solution.py:640
  87.3 1.0 %reshape.55 = bf16[32,4,2048]{2,1,0:T(4,128)(2,1)} reshape(bf16[128,2048]{1,0:T(8,128)(2,1)S(1)} %return_rows.1) | data formatting | bytes 1048576 | tf_op jit(solution)/shard_map/reshape | solution.py:656
  (8 shorter events, 0.0 us)
Async XLA Ops:
  3.0 0.7 copy-start.9
  3.6 0.7 copy-start.10
  4.3 0.7 copy-start.11
  21.5 0.9 %copy-start.2 = (bf16[2048,32]{0,1:T(8,128)(2,1)S(1)}, bf16[2048,32]{0,1:T(8,128)(2,1)}, u32[]{:S(2)}) copy-start(bf16[2048,32]{0,1:T(8,128)(2,1)} %param.26) | copy-start | bytes 393220
  22.4 0.8 copy-start.4
  23.2 0.7 copy-start.5
  23.9 7.2 %copy-start = (bf16[1024,512]{1,0:T(8,128)(2,1)S(1)}, bf16[1024,512]{1,0:T(8,128)(2,1)}, u32[]{:S(2)}) copy-start(bf16[1024,512]{1,0:T(8,128)(2,1)} %up_ref.2) | copy-start | bytes 3145732
  23.9 7.2 %copy-start.8 = (f32[512]{0:T(512)S(1)}, f32[512]{0:T(512)}, u32[]{:S(2)}) copy-start(f32[512]{0:T(512)} %param.29) | copy-start | bytes 6148
  23.9 30.7 %copy-start.3 = (f32[16,2048]{1,0:T(8,128)S(1)}, f32[16,2048]{1,0:T(8,128)}, u32[]{:S(2)}) copy-start(f32[16,2048]{1,0:T(8,128)} %rate_ref.1) | copy-start | bytes 393220
  23.9 30.7 %copy-start.6 = (f32[2048]{0:T(1024)S(1)}, f32[2048]{0:T(1024)}, u32[]{:S(2)}) copy-start(f32[2048]{0:T(1024)} %param.31) | copy-start | bytes 24580
  23.9 30.7 %copy-start.7 = (f32[2048]{0:T(1024)S(1)}, f32[2048]{0:T(1024)}, u32[]{:S(2)}) copy-start(f32[2048]{0:T(1024)} %param.33) | copy-start | bytes 24580
  53.6 1.0 %copy-start.1 = (bf16[8,32,2048]{2,1,0:T(8,128)(2,1)}, bf16[8,32,2048]{2,1,0:T(8,128)(2,1)S(1)}, u32[]{:S(2)}) copy-start(bf16[8,32,2048]{2,1,0:T(8,128)(2,1)S(1)} %get-tuple-element.23.gate_ref) | copy-start | bytes 3145732

commit v4 on v3

--- a/solution.py
+++ b/solution.py
@@ -11,7 +11,7 @@
 ADAPTER_RANK = 16
 TENANT_COUNT = 64
 LABELS = 128
-VMEM_BYTES = 50 * 1024 * 1024
+MIB = 1024 * 1024
 LOG2_E = 1.4426950408889634
 F32 = jnp.float32
 BF16 = jnp.bfloat16
@@ -117,9 +117,10 @@
 
 def pick_rows(selector, rows_ref, out_ref, offset=0):
     owners, block, _ = out_ref.shape
-    for at in range(0, rows_ref.shape[1], 512):
-        wide = min(512, rows_ref.shape[1] - at)
-        part = jnp.dot(selector, rows_ref[:, at : at + wide], preferred_element_type=F32)
+    for at in range(0, rows_ref.shape[2], 512):
+        wide = min(512, rows_ref.shape[2] - at)
+        rows = rows_ref[:, :, at : at + wide].astype(F32).reshape(selector.shape[1], wide)
+        part = jnp.dot(selector, rows.astype(BF16), preferred_element_type=F32)
         out_ref[:, :, at : at + wide] = part.reshape(owners, block, wide).astype(BF16)
 
 
@@ -142,8 +143,8 @@
     picked = dispatch_matrix(holder_ref[...], owners, per_owner, steps)
     selector = picked.astype(BF16)
     back_ref[...] = picked.T.astype(BF16)
-    lanes = rows_ref.shape[0]
-    chans = rows_ref.shape[1]
+    lanes = rows_ref.shape[0] * steps
+    chans = rows_ref.shape[2]
     slots = owners * per_owner
     line = iota((LABELS, lanes), 0).astype(F32)
     labels = as_bf16(
@@ -429,11 +430,10 @@
     for copy in spread(result_ref, landed, send_sem, recv_sem, local_sem, "pool", owners):
         copy.wait()
     total = back_ref.shape[1]
-    for at in range(0, out_ref.shape[1], 512):
+    for at in range(0, out_ref.shape[2], 512):
         rows = landed[:, :, at : at + 512].astype(F32).reshape(total, 512).astype(BF16)
-        out_ref[:, at : at + 512] = jnp.dot(
-            back_ref[...], rows, preferred_element_type=F32
-        ).astype(BF16)
+        part = jnp.dot(back_ref[...], rows, preferred_element_type=F32)
+        out_ref[:, :, at : at + 512] = part.reshape(out_ref.shape[:2] + (512,)).astype(BF16)
 
 
 def local(
@@ -471,8 +471,6 @@
     holder = session_holder.reshape(1, served)
     slot = session_slot.reshape(1, served)
     tenant = conversation_customer.reshape(1, served)
-    mixer = projected_mixer.reshape(lanes, chans)
-    gate = projected_gate.reshape(lanes, chans)
     cache = jnp.swapaxes(slot_state_cache, 0, 1)
     maps_weight = state_maps_weight.T
 
@@ -494,10 +492,11 @@
             dma,
         ],
         compiler_params=pltpu.CompilerParams(
-            collective_id=0, has_side_effects=True, vmem_limit_bytes=VMEM_BYTES
-        ),
+            collective_id=0, has_side_effects=True, vmem_limit_bytes=10 * MIB
+        ),
+        cost_estimate=pl.CostEstimate(flops=0, bytes_accessed=60 * MIB, transcendentals=0),
         name="send_rows",
-    )(holder, slot, tenant, mixer)
+    )(holder, slot, tenant, projected_mixer)
 
     wide = min(512, chans)
     part, by_slot, act, to_arrival, to_slot, mask = pl.pallas_call(
@@ -535,7 +534,8 @@
             pltpu.VMEM((total, LABELS), F32),
             pltpu.VMEM((total, ranks), F32),
         ],
-        compiler_params=pltpu.CompilerParams(vmem_limit_bytes=VMEM_BYTES),
+        compiler_params=pltpu.CompilerParams(vmem_limit_bytes=50 * MIB),
+        cost_estimate=pl.CostEstimate(flops=0, bytes_accessed=26 * MIB, transcendentals=0),
         name="project",
     )(
         arrived,
@@ -575,12 +575,13 @@
             dma((2,)),
         ],
         compiler_params=pltpu.CompilerParams(
-            collective_id=1, has_side_effects=True, vmem_limit_bytes=VMEM_BYTES
-        ),
+            collective_id=1, has_side_effects=True, vmem_limit_bytes=14 * MIB
+        ),
+        cost_estimate=pl.CostEstimate(flops=0, bytes_accessed=74 * MIB, transcendentals=0),
         name="join",
     )(
         holder,
-        gate,
+        projected_gate,
         part,
         mask.reshape(tp_count, share, LABELS),
         adapter_up_maps,
@@ -620,7 +621,8 @@
             pltpu.VMEM((slots, LABELS), F32),
             pltpu.VMEM((STATE, wide), F32),
         ],
-        compiler_params=pltpu.CompilerParams(vmem_limit_bytes=VMEM_BYTES),
+        compiler_params=pltpu.CompilerParams(vmem_limit_bytes=36 * MIB),
+        cost_estimate=pl.CostEstimate(flops=0, bytes_accessed=65 * MIB, transcendentals=0),
         name="scan",
     )(
         normed.reshape(total, rank),
@@ -639,7 +641,7 @@
 
     gated = pl.pallas_call(
         functools.partial(return_rows, owners),
-        out_shape=shape((lanes, chans), BF16),
+        out_shape=shape((served, steps, chans), BF16),
         in_specs=[whole_vmem()] * 2,
         out_specs=whole_vmem(),
         scratch_shapes=[
@@ -649,11 +651,12 @@
             dma,
         ],
         compiler_params=pltpu.CompilerParams(
-            collective_id=2, has_side_effects=True, vmem_limit_bytes=VMEM_BYTES
-        ),
+            collective_id=2, has_side_effects=True, vmem_limit_bytes=8 * MIB
+        ),
+        cost_estimate=pl.CostEstimate(flops=0, bytes_accessed=55 * MIB, transcendentals=0),
         name="return_rows",
     )(back, result)
-    return (gated.reshape(served, steps, chans), jnp.swapaxes(new_cache, 0, 1))
+    return (gated, jnp.swapaxes(new_cache, 0, 1))
 
 
 def solution(mesh):

time: 89.3 us -> 86.1 us (0.964)
  local copies, waits for them, and re-layouts: 8.62 us -> 6.61 us
  Pallas kernels: 78.9 us -> 77.8 us
    reshape x3 -> x0, local copies, waits for them, and re-layouts: 3.31 us -> none  [the longest x1 1.16 us: local(): gate = projected_gate.reshape(lanes, chans)]
    unnamed x24 -> x35, local copies, waits for them, and re-layouts: 5.31 us -> 6.61 us
    pallas_call x1, Pallas kernels: 18.8 us -> 17.7 us  [local(): pl.pallas_call(functools.partial(scan, steps), grid=(chans // wide,), out...]
where the time goes in v4:
time: 86.1 us; the launch traced here: 85.3 us
  Pallas kernels  77.8 us (90%)
  local copies, waits for them, and re-layouts  6.61 us (8%)
    pallas_call x1, Pallas kernels, local(): pl.pallas_call(functools.partial(join, owners, per_owner, steps, tp_count...  22.5 us
    pallas_call x1, Pallas kernels, local(): pl.pallas_call(functools.partial(scan, steps), grid=(chans // wide,), out...  17.7 us
    pallas_call x1, Pallas kernels, local(): pl.pallas_call(functools.partial(send_rows, owners, per_owner, steps), ou...  16.6 us
    pallas_call x1, Pallas kernels, local(): pl.pallas_call(functools.partial(return_rows, owners), out_shape=shape((s...  13.9 us
    pallas_call x1, Pallas kernels, local(): pl.pallas_call(functools.partial(project, steps, tp_count), grid=(chans /...  7.16 us
    unnamed x35, local copies, waits for them, and re-layouts  6.61 us

profile of v4, /device:TPU:0, one launch (start us, length us, event | category | flops | bytes accessed | tf_op | source)
XLA Modules:
  0.0 85.3 jit_solution(18248362500103985421)
XLA Ops:
  0.6 0.0 copy-start.3
  0.6 1.0 %copy-done.3 = bf16[32,4,2048]{2,1,0:T(4,128)(2,1)S(1)} copy-done((bf16[32,4,2048]{2,1,0:T(4,128)(2,1)S(1)}, bf16[32,4,2048]{2,1,0:T(4,128)(2,1)}, u32[]{:S(2)}) %copy-start.3) | copy-done | bytes 524312
  1.7 0.7 copy-done.11
  2.3 0.7 copy-done.13
  3.0 0.7 copy-done.14
  3.6 16.6 %send_rows.1 = (bf16[8,32,2176]{2,1,0:T(8,128)(2,1)S(1)}, bf16[128,256]{1,0:T(8,128)(2,1)S(1)}) custom-call(s32[1,32]{1,0:T(1,128)S(1)} %bitcast.27, s32[1,32]{1,0:T(1,128)S(1)} %bitcast.29, s32[1,32]{1,0:T(1,128)S(1)} %bitcast.30, bf16[32,4,2048]{2,1,0:T(4,128)(2,1)S(1)} %copy-done.3), custom_call_target="tpu_custom_call" | custom-call | bytes 62914560 | tf_op jit(solution)/shard_map/send_rows/pallas_call | solution.py:480
  20.2 0.0 slice-start
  20.2 0.0 copy-start.4
  20.2 1.0 %copy-done.4 = bf16[2048,32]{0,1:T(8,128)(2,1)S(1)} copy-done((bf16[2048,32]{0,1:T(8,128)(2,1)S(1)}, bf16[2048,32]{0,1:T(8,128)(2,1)}, u32[]{:S(2)}) %copy-start.4) | copy-done | bytes 131096
  21.3 1.0 %copy-done.6 = f32[4,2048]{1,0:T(4,128)S(1)} copy-done((f32[4,2048]{1,0:T(4,128)S(1)}, f32[4,2048]{1,0:T(4,128)}, u32[]{:S(2)}) %copy-start.6) | copy-done | bytes 32792
  22.3 0.7 copy-done.7
  23.0 0.0 slice-start.1
  23.0 0.0 copy-start
  23.0 0.0 copy-start.5
  23.0 0.0 copy-start.8
  23.0 0.0 copy-start.9
  23.1 7.2 %project.1 = (bf16[4,64,640]{2,1,0:T(8,128)(2,1)S(1)}, bf16[256,2048]{1,0:T(8,128)(2,1)S(1)}, bf16[256,2048]{1,0:T(8,128)(2,1)S(1)}, bf16[256,256]{1,0:T(8,128)(...) custom-call(bf16[8,32,2176]{2,1,0:T(8,128)(2,1)S(1)} %get-tuple-element.16.arrived_ref, ...), custom_call_target="tpu_custom_call" | custom-call | bytes 27262976 | tf_op jit(solution)/shard_map/project/pallas_call | solution.py:502
  30.2 0.0 copy-done.1
  30.2 0.0 copy-done.2
  30.2 0.0 copy-done.10
  30.3 22.5 %join.1 = (bf16[8,32,2048]{2,1,0:T(8,128)(2,1)S(1)}, bf16[4,64,512]{2,1,0:T(8,128)(2,1)S(1)}, f32[4,64,128]{2,1,0:T(8,128)S(1)}) custom-call(s32[1,32]{1,0:T(1,128)S(1)} %bitcast.28, bf16[32,4,2048]{2,1,0:T(4,128)(2,1)S(1)} %copy-done.2, bf16[4,64,640]{2,1,0:T(8,128)(2,1)S(1)} %get-tuple-element.17.part_ref, bf16[4,64,128]{2,1,0:T(8,128)(2,1)S(1)} %bitcast.22, ...), custom_call_target="tpu_custom_call" | custom-call | bytes 77594624 | tf_op jit(solution)/shard_map/join/pallas_call | solution.py:552
  52.9 17.7 %scan.1 = (bf16[19,64,2048]{2,1,0:T(8,128)(2,1)}, bf16[8,32,2048]{2,1,0:T(8,128)(2,1)S(1)}) custom-call(bf16[256,512]{1,0:T(8,128)(2,1)S(1)} %bitcast.19, f32[256,128]{1,0:T(8,128)S(1)} %bitcast.21, bf16[512,2048]{1,0:T(8,128)(2,1)S(1)} %copy-done, f32[1,2048]{1,0:T(1,128)S(1)} %bitcast.24, f32[16,2048]{1,0:T(8,128)S(1)} %copy-done.5, ...), custom_call_target="tpu_custom_call" | custom-call | bytes 68157440 | tf_op jit(solution)/shard_map/scan/pallas_call | solution.py:591
  70.6 13.9 %return_rows.1 = bf16[32,4,2048]{2,1,0:T(4,128)(2,1)S(1)} custom-call(bf16[128,256]{1,0:T(8,128)(2,1)S(1)} %get-tuple-element.15.back_ref, bf16[8,32,2048]{2,1,0:T(8,128)(2,1)S(1)} %get-tuple-element.26.result_ref), custom_call_target="tpu_custom_call" | custom-call | bytes 57671680 | tf_op jit(solution)/shard_map/return_rows/pallas_call | solution.py:642
  84.5 0.8 copy.20
  (17 shorter events, 0.0 us)
Async XLA Ops:
  0.6 1.0 %copy-start.3 = (bf16[32,4,2048]{2,1,0:T(4,128)(2,1)S(1)}, bf16[32,4,2048]{2,1,0:T(4,128)(2,1)}, u32[]{:S(2)}) copy-start(bf16[32,4,2048]{2,1,0:T(4,128)(2,1)} %rows_ref.1) | copy-start | bytes 1572868
  1.7 0.7 copy-start.11
  2.3 0.7 copy-start.13
  3.0 0.7 copy-start.14
  20.2 32.6 %slice-start = ((s8[4980736]{0:T(1024)(128)(4,1)}), s8[4194304]{0:T(1024)(128)(4,1)S(1)}, s32[]{:S(2)}) async-start(s8[4980736]{0:T(1024)(128)(4,1)} %bitcast.16), calls=%async_computation | async-start | bytes 8388608
  20.2 1.1 %copy-start.4 = (bf16[2048,32]{0,1:T(8,128)(2,1)S(1)}, bf16[2048,32]{0,1:T(8,128)(2,1)}, u32[]{:S(2)}) copy-start(bf16[2048,32]{0,1:T(8,128)(2,1)} %param.26) | copy-start | bytes 393220
  21.3 1.0 %copy-start.6 = (f32[4,2048]{1,0:T(4,128)S(1)}, f32[4,2048]{1,0:T(4,128)}, u32[]{:S(2)}) copy-start(f32[4,2048]{1,0:T(4,128)} %tap_ref.1) | copy-start | bytes 98308
  22.3 0.7 copy-start.7
  23.0 7.2 %copy-start.1 = (bf16[1024,512]{1,0:T(8,128)(2,1)S(1)}, bf16[1024,512]{1,0:T(8,128)(2,1)}, u32[]{:S(2)}) copy-start(bf16[1024,512]{1,0:T(8,128)(2,1)} %up_ref.2) | copy-start | bytes 3145732
  23.0 7.2 %copy-start.2 = (bf16[32,4,2048]{2,1,0:T(4,128)(2,1)S(1)}, bf16[32,4,2048]{2,1,0:T(4,128)(2,1)}, u32[]{:S(2)}) copy-start(bf16[32,4,2048]{2,1,0:T(4,128)(2,1)} %gate_ref.1) | copy-start | bytes 1572868
  23.0 7.3 %copy-start.10 = (f32[512]{0:T(512)S(1)}, f32[512]{0:T(512)}, u32[]{:S(2)}) copy-start(f32[512]{0:T(512)} %param.29) | copy-start | bytes 6148
  23.0 7.3 %copy-start.12 = (s32[32]{0:T(128)S(1)}, s32[32]{0:T(128)}, u32[]{:S(2)}) copy-start(s32[32]{0:T(128)} %param.20) | copy-start | bytes 388
  23.0 29.8 %slice-start.1 = ((s8[4980736]{0:T(1024)(128)(4,1)}), s8[786432]{0:T(1024)(128)(4,1)S(1)}, s32[]{:S(2)}) async-start(s8[4980736]{0:T(1024)(128)(4,1)} %bitcast.16), calls=%async_computation.1 | async-start | bytes 1572864
  23.0 29.8 %copy-start = (bf16[512,2048]{1,0:T(8,128)(2,1)S(1)}, bf16[512,2048]{1,0:T(8,128)(2,1)}, u32[]{:S(2)}) copy-start(bf16[512,2048]{1,0:T(8,128)(2,1)} %up_ref.3) | copy-start | bytes 6291460
  23.0 29.8 %copy-start.5 = (f32[16,2048]{1,0:T(8,128)S(1)}, f32[16,2048]{1,0:T(8,128)}, u32[]{:S(2)}) copy-start(f32[16,2048]{1,0:T(8,128)} %rate_ref.1) | copy-start | bytes 393220
  23.0 29.8 %copy-start.8 = (f32[2048]{0:T(1024)S(1)}, f32[2048]{0:T(1024)}, u32[]{:S(2)}) copy-start(f32[2048]{0:T(1024)} %param.31) | copy-start | bytes 24580
  23.0 29.8 %copy-start.9 = (f32[2048]{0:T(1024)S(1)}, f32[2048]{0:T(1024)}, u32[]{:S(2)}) copy-start(f32[2048]{0:T(1024)} %param.33) | copy-start | bytes 24580
